TPU v7x, 512 devices: a whole 4x4x16 slice. The times are simulated.
512 devices in a mesh: dp: 64 (over x, z), et: 8 (over y, core).
Axes of the slice: x: 4, y: 4, z: 16, core: 2. Of those that a mesh axis runs over, the one named last changes fastest.
Arguments:
- token_rows: bfloat16 [16384, 3072], P(('dp', 'et')), may hold values from -6 to 6
- route_weight: float32 [16384], P(('dp', 'et')), may hold values from 0.05 to 1
- live_count: int32 [512], P(('dp', 'et')), may hold values from 1 to 32, as said below
- gate_pre: bfloat16 [16384, 8192], P('dp', 'et'), may hold values from -10 to 10
- up_pre: bfloat16 [16384, 8192], P('dp', 'et'), may hold values from -6 to 6
- hidden_grad: bfloat16 [16384, 8192], P('dp', 'et'), may hold values from -6 to 6
Outputs:
- gate_grad: float32 [3072, 8192], P('dp', 'et')
Inputs may be any that keep to these rules, and one draw needn't show every extreme that they name: The first live_count slots of each device are live. Some device has exactly 32 and some exactly 1.
All inputs are finite; a program needn't handle non-finite values.
Results may differ from a plain program's by a relative error of at most 0.004.
Values may be sent and summed in bfloat16 or wider, within the bound.
No kernel may reach another device: no remote copies, remote signals or barrier semaphores. Data moves between devices by JAX's collectives and lax.ppermute only.
A program may use at most 128 MiB of HBM per device.

v0:
```python
import math

import jax
import jax.numpy as jnp
from jax import lax
from jax.sharding import PartitionSpec as P


def swapped(value, axis, bit):
    return lax.ppermute(value, axis, [(i, i ^ 1 << bit) for i in range(lax.axis_size(axis))])


def gate_slope(gate_pre, up_pre, hidden_grad):
    gate_value = gate_pre.astype(jnp.float32)
    sigmoid_v = jax.nn.sigmoid(gate_value)
    silu_slope = sigmoid_v * (1.0 + gate_value * (1.0 - sigmoid_v))
    return (hidden_grad.astype(jnp.float32) * up_pre.astype(jnp.float32) * silu_slope).astype(
        jnp.bfloat16
    )


def row_product(left_rows, right_rows):
    return lax.dot_general(
        left_rows, right_rows, (((0,), (0,)), ((), ())), preferred_element_type=jnp.float32
    )


def shards(token_rows, route_weight, live_count, gate_pre, up_pre, hidden_grad):
    row_count = token_rows.shape[0]
    feature_count = token_rows.shape[1]
    live_rows = jnp.arange(row_count, dtype=jnp.int32) < live_count[0]
    factor_rows = route_weight * live_rows.astype(jnp.float32)
    weighted = (token_rows.astype(jnp.float32) * factor_rows[:, None]).astype(jnp.bfloat16)
    gate_delta = gate_slope(gate_pre, up_pre, hidden_grad)
    unit_count = gate_delta.shape[1]
    local_grad = row_product(lax.all_gather(weighted, "et", axis=0, tiled=True), gate_delta)
    dp_size = lax.axis_size("dp")
    level_total = dp_size.bit_length() - 1
    own_index = lax.axis_index("dp")
    shard_count = feature_count // dp_size
    pending = local_grad.reshape(dp_size, shard_count, unit_count)
    for level_bit in reversed(range(level_total)):
        own_bit = own_index >> level_bit & 1
        paired = pending.reshape(2, pending.shape[0] // 2, shard_count, unit_count)
        kept_half = lax.dynamic_index_in_dim(paired, own_bit, 0, keepdims=False)
        sent_half = lax.dynamic_index_in_dim(paired, 1 - own_bit, 0, keepdims=False)
        pending = kept_half + swapped(sent_half, "dp", level_bit)
    owned = pending.reshape(shard_count, unit_count)
    norm_factor = 1.0 / math.sqrt(row_count * dp_size * lax.axis_size("et"))
    return owned * norm_factor


def solution(mesh):
    placed = (
        P(("dp", "et"), None),
        P(("dp", "et")),
        P(("dp", "et")),
        P("dp", "et"),
        P("dp", "et"),
        P("dp", "et"),
    )
    return jax.shard_map(
        shards, mesh=mesh, in_specs=placed, out_specs=P("dp", "et"), check_vma=False
    )
```

profile of v0, /device:TPU:6, one launch (start us, length us, event | category | flops | bytes accessed | tf_op | source)
XLA Modules:
  0.0 532.2 jit_solution(6612897262144922723)
XLA Ops:
  6.5 0.0 all-gather.2.cloned.1.call-start
  7.2 0.7 compare_select_fusion
  7.8 1.7 multiply_convert_fusion
  9.6 0.0 all-gather.2.cloned.1.call-update
  9.6 36.6 %all-gather.2.cloned.1.call-done = bf16[256,3072]{1,0:T(8,128)(2,1)} async-done(((bf16[32,3072]{1,0:T(8,128)(2,1)}), bf16[256,3072]{1,0:T(8,128)(2,1)}) %all-gather.2.cloned.1.call-update) | async-done | bytes 1572880 | tf_op jit(solution)/shard_map/all_gather | solution.py:36
  46.2 3.9 fusion.7
  50.0 0.0 copy-start
  50.0 3.6 dynamic-slice_bitcast_fusion
  53.6 2.9 copy-done
  56.5 3.3 collective-permute-start
  59.9 138.0 %collective-permute-done = f32[32,48,1024]{2,1,0:T(8,128)} collective-permute-done((f32[32,48,1024]{2,1,0:T(8,128)}, f32[32,48,1024]{2,1,0:T(8,128)}, u32[]{:S(2)}, u32[]{:S(2)}) %collective-permute-start) | collective-permute-done | bytes 6291488 | tf_op jit(solution)/shard_map/ppermute | solution.py:10
  197.9 6.1 %bitcast_add_fusion = f32[32,48,1024]{2,1,0:T(8,128)S(1)} fusion(f32[32,48,1024]{2,1,0:T(8,128)} %collective-permute-done, f32[2,32,48,1024]{3,2,1,0:T(8,128)} %bitcast.31, s32[]{:T(128)S(6)} %select_n.42), kind=kLoop, calls=%fused_computation | loop fusion | flops 1572864 | bytes 18874372 | tf_op jit(solution)/shard_map/add | solution.py:47
  204.0 0.0 copy-start.1
  204.0 0.2 dynamic-slice_bitcast_fusion.1
  204.2 2.4 copy-done.1
  206.6 2.7 collective-permute-start.1
  209.4 68.7 %collective-permute-done.1 = f32[16,48,1024]{2,1,0:T(8,128)} collective-permute-done((f32[16,48,1024]{2,1,0:T(8,128)S(1)}, f32[16,48,1024]{2,1,0:T(8,128)}, u32[]{:S(2)}, u32[]{:S(2)}) %collective-permute-start.1) | collective-permute-done | bytes 3145760 | tf_op jit(solution)/shard_map/ppermute | solution.py:10
  278.1 3.5 bitcast_add_fusion.1
  281.6 1.3 dynamic-slice_bitcast_fusion.2
  282.9 12.8 %collective-permute-start.2 = (f32[8,48,1024]{2,1,0:T(8,128)}, f32[8,48,1024]{2,1,0:T(8,128)}, u32[]{:S(2)}, u32[]{:S(2)}) collective-permute-start(f32[8,48,1024]{2,1,0:T(8,128)} %dynamic-slice_bitcast_fusion.2), channel_id=1, source_target_pairs={{0,64},{8,72},{16,80},{24,88},{32,96},{40,104},{48,112},{56,120},{... | collective-permute-start | bytes 4718600 | tf_op jit(solution)/shard_map/ppermute | solution.py:10
  295.7 133.9 %collective-permute-done.2 = f32[8,48,1024]{2,1,0:T(8,128)} collective-permute-done((f32[8,48,1024]{2,1,0:T(8,128)}, f32[8,48,1024]{2,1,0:T(8,128)}, u32[]{:S(2)}, u32[]{:S(2)}) %collective-permute-start.2) | collective-permute-done | bytes 1572896 | tf_op jit(solution)/shard_map/ppermute | solution.py:10
  429.6 1.7 bitcast_add_fusion.2
  431.3 1.1 copy-done.2
  432.4 0.1 dynamic-slice_bitcast_fusion.3
  432.5 8.3 %collective-permute-start.3 = (f32[4,48,1024]{2,1,0:T(8,128)S(1)}, f32[4,48,1024]{2,1,0:T(8,128)S(1)}, u32[]{:S(2)}, u32[]{:S(2)}) collective-permute-start(f32[4,48,1024]{2,1,0:T(8,128)S(1)} %dynamic-slice_bitcast_fusion.3), channel_id=1, source_target_pairs={{0,32},{8,40},{16,48},{24,56},{32,0},{40,8},{48,16},{56,24},{64,96... | collective-permute-start | bytes 2359304 | tf_op jit(solution)/shard_map/ppermute | solution.py:10
  440.8 57.3 %collective-permute-done.3 = f32[4,48,1024]{2,1,0:T(8,128)S(1)} collective-permute-done((f32[4,48,1024]{2,1,0:T(8,128)S(1)}, f32[4,48,1024]{2,1,0:T(8,128)S(1)}, u32[]{:S(2)}, u32[]{:S(2)}) %collective-permute-start.3) | collective-permute-done | bytes 786464 | tf_op jit(solution)/shard_map/ppermute | solution.py:10
  498.1 1.2 bitcast_add_fusion.3
  499.4 1.9 collective-permute-start.4
  501.3 15.7 %collective-permute-done.4 = f32[2,48,1024]{2,1,0:T(8,128)S(1)} collective-permute-done((f32[2,48,1024]{2,1,0:T(8,128)S(1)}, f32[2,48,1024]{2,1,0:T(8,128)S(1)}, u32[]{:S(2)}, u32[]{:S(2)}) %collective-permute-start.4) | collective-permute-done | bytes 393248 | tf_op jit(solution)/shard_map/ppermute | solution.py:10
  517.1 1.9 collective-permute-start.5
  519.0 5.6 %collective-permute-done.5 = f32[1,48,1024]{2,1,0:T(8,128)S(1)} collective-permute-done((f32[1,48,1024]{2,1,0:T(8,128)S(1)}, f32[1,48,1024]{2,1,0:T(8,128)S(1)}, u32[]{:S(2)}, u32[]{:S(2)}) %collective-permute-start.5) | collective-permute-done | bytes 196640 | tf_op jit(solution)/shard_map/ppermute | solution.py:10
  524.6 0.7 multiply_bitcast_fusion
  (4 shorter events, 0.1 us)
Async XLA Ops:
  6.5 39.6 %all-gather.2.cloned.1.call-start = ((), (), s32[]{:S(2)}) async-start(), calls=%async_computation | async-start | bytes 1769472 | tf_op jit(solution)/shard_map/all_gather | solution.py:36
  50.0 6.5 %copy-start = (f32[3072,1024]{1,0:T(8,128)}, f32[3072,1024]{1,0:T(8,128)S(1)}, u32[]{:S(2)}) copy-start(f32[3072,1024]{1,0:T(8,128)S(1)} %fusion.7) | copy-start | bytes 37748740
  56.5 141.4 %collective-permute-start = (f32[32,48,1024]{2,1,0:T(8,128)}, f32[32,48,1024]{2,1,0:T(8,128)}, u32[]{:S(2)}, u32[]{:S(2)}) collective-permute-start(f32[32,48,1024]{2,1,0:T(8,128)} %dynamic-slice_bitcast_fusion), channel_id=1, source_target_pairs={{0,256},{8,264},{16,272},{24,280},{32,288},{40,296},{48,304},{56,3... | collective-permute-start | bytes 18874376 | tf_op jit(solution)/shard_map/ppermute | solution.py:10
  204.0 2.7 copy-start.1
  206.6 71.4 %collective-permute-start.1 = (f32[16,48,1024]{2,1,0:T(8,128)S(1)}, f32[16,48,1024]{2,1,0:T(8,128)}, u32[]{:S(2)}, u32[]{:S(2)}) collective-permute-start(f32[16,48,1024]{2,1,0:T(8,128)S(1)} %dynamic-slice_bitcast_fusion.1), channel_id=1, source_target_pairs={{0,128},{8,136},{16,144},{24,152},{32,160},{40,168},{48,176},{56,1... | collective-permute-start | bytes 9437192 | tf_op jit(solution)/shard_map/ppermute | solution.py:10
  282.9 146.8 %collective-permute-start.2 = (f32[8,48,1024]{2,1,0:T(8,128)}, f32[8,48,1024]{2,1,0:T(8,128)}, u32[]{:S(2)}, u32[]{:S(2)}) collective-permute-start(f32[8,48,1024]{2,1,0:T(8,128)} %dynamic-slice_bitcast_fusion.2), channel_id=1, source_target_pairs={{0,64},{8,72},{16,80},{24,88},{32,96},{40,104},{48,112},{56,120},{... | collective-permute-start | bytes 4718600 | tf_op jit(solution)/shard_map/ppermute | solution.py:10
  431.3 1.2 copy-start.2
  432.5 65.6 %collective-permute-start.3 = (f32[4,48,1024]{2,1,0:T(8,128)S(1)}, f32[4,48,1024]{2,1,0:T(8,128)S(1)}, u32[]{:S(2)}, u32[]{:S(2)}) collective-permute-start(f32[4,48,1024]{2,1,0:T(8,128)S(1)} %dynamic-slice_bitcast_fusion.3), channel_id=1, source_target_pairs={{0,32},{8,40},{16,48},{24,56},{32,0},{40,8},{48,16},{56,24},{64,96... | collective-permute-start | bytes 2359304 | tf_op jit(solution)/shard_map/ppermute | solution.py:10
  499.4 17.6 %collective-permute-start.4 = (f32[2,48,1024]{2,1,0:T(8,128)S(1)}, f32[2,48,1024]{2,1,0:T(8,128)S(1)}, u32[]{:S(2)}, u32[]{:S(2)}) collective-permute-start(f32[2,48,1024]{2,1,0:T(8,128)S(1)} %dynamic-slice_bitcast_fusion.4), channel_id=1, source_target_pairs={{0,16},{8,24},{16,0},{24,8},{32,48},{40,56},{48,32},{56,40},{64,80... | collective-permute-start | bytes 1179656 | tf_op jit(solution)/shard_map/ppermute | solution.py:10
  517.1 7.6 %collective-permute-start.5 = (f32[1,48,1024]{2,1,0:T(8,128)S(1)}, f32[1,48,1024]{2,1,0:T(8,128)S(1)}, u32[]{:S(2)}, u32[]{:S(2)}) collective-permute-start(f32[1,48,1024]{2,1,0:T(8,128)S(1)} %constant_dynamic-slice_fusion), channel_id=1, source_target_pairs={{0,8},{8,0},{16,24},{24,16},{32,40},{40,32},{48,56},{56,48},{64,72... | collective-permute-start | bytes 589832 | tf_op jit(solution)/shard_map/ppermute | solution.py:10
Sparse Core Ops, SparseCore 0:
  9.7 36.4 all-gather.1
where the time goes:
time: 536 us; the launch traced here: 532 us
  waiting for transfers between devices  456 us (85%)
  starting transfers between devices  31 us (6%)
  other arithmetic  15.6 us (3%)
  between operations  14.2 us (3%)
  local copies, waits for them, and re-layouts  11.7 us (2%)
    ppermute x6, waiting for transfers between devices, swapped(): lax.ppermute(value, axis, [(i, i ^ 1 << bit) for i in range(lax.axis_size...  419 us
    all_gather x1, waiting for transfers between devices, shards(): lax.all_gather(weighted, 'et', axis=0, tiled=True)  36.6 us
    ppermute x6, starting transfers between devices, swapped(): lax.ppermute(value, axis, [(i, i ^ 1 << bit) for i in range(lax.axis_size...  31 us
    add x5, other arithmetic, shards(): pending = kept_half + swapped(sent_half, 'dp', level_bit)  12.5 us
  transfers between devices with their start and end apart: 7, of which 7 were waited for; matrix products, arithmetic and copies ran while one was open for 0% of the time, Pallas kernels for 0%

commit v1 on v0

v1 whole, which is shorter than its diff:
```python
import math

import jax
import jax.numpy as jnp
from jax import lax
from jax.sharding import Mesh, PartitionSpec as P

X, ZH, ZL, Y, C = 4, 4, 4, 4, 2
Z = ("zh", "zl")
DP = ("x", "zh", "zl")
ET = ("y", "c")


def gate_slope(gate_pre, up_pre, hidden_grad):
    gate_value = gate_pre.astype(jnp.float32)
    sigmoid_v = jax.nn.sigmoid(gate_value)
    silu_slope = sigmoid_v * (1.0 + gate_value * (1.0 - sigmoid_v))
    return (hidden_grad.astype(jnp.float32) * up_pre.astype(jnp.float32) * silu_slope).astype(
        jnp.bfloat16
    )


def z_shift(value, step):
    return lax.ppermute(value, Z, [(i, (i + step) % (ZH * ZL)) for i in range(ZH * ZL)])


def pick(value, index, axis):
    return lax.dynamic_index_in_dim(value, index, axis, keepdims=False)


def f32(value):
    return value.astype(jnp.float32)


def shards(token_rows, route_weight, live_count, gate_pre, up_pre, hidden_grad):
    rows, features = token_rows.shape
    units = gate_pre.shape[1]
    part = features // X
    owned = part // (ZH * ZL)
    core = lax.axis_index("c")
    zl = lax.axis_index("zl")

    delta = gate_slope(gate_pre, up_pre, hidden_grad).reshape(Y, C, rows, units)
    delta = jnp.stack([pick(delta, core, 1), pick(delta, 1 - core, 1)])
    delta = lax.all_gather(delta.reshape(C * Y * rows, units), "x", axis=0, tiled=False)

    live_rows = jnp.arange(rows, dtype=jnp.int32) < live_count[0]
    factor_rows = route_weight * live_rows.astype(jnp.float32)
    weighted = (f32(token_rows) * factor_rows[:, None]).astype(jnp.bfloat16)
    parts = weighted.reshape(rows, X, part).transpose(1, 0, 2)
    parts = jnp.broadcast_to(parts[:, None], (X, Y, rows, part)).reshape(X * Y, rows, part)
    own = lax.all_to_all(parts, ("x", "y"), 0, 0)
    other = lax.ppermute(own, "c", [(0, 1), (1, 0)])
    tokens = jnp.stack(
        [own.reshape(X, Y * rows, part), other.reshape(X, Y * rows, part)], axis=1
    )

    product = lax.dot_general(
        tokens.reshape(X * C * Y * rows, part),
        delta.reshape(X * C * Y * rows, units),
        (((0,), (0,)), ((), ())),
        preferred_element_type=jnp.float32,
    ).reshape(ZH, ZL, owned, units)

    half = units // 2
    above = pick(product, (zl + 1) % ZL, 1).astype(jnp.bfloat16)
    below = pick(product, (zl + 3) % ZL, 1).astype(jnp.bfloat16)
    across = pick(product, (zl + 2) % ZL, 1).astype(jnp.bfloat16)
    total = pick(product, zl, 1)
    far = jnp.concatenate(
        [f32(z_shift(across[..., :half], -2)), f32(z_shift(across[..., half:], 2))], axis=-1
    )
    total = total + f32(z_shift(above, 1)) + f32(z_shift(below, -1)) + far

    arrived = lax.all_to_all(total.astype(jnp.bfloat16), "zh", 0, 0)
    count = rows * X * ZH * ZL * Y * C
    return f32(arrived).sum(0) * (1.0 / math.sqrt(count))


def solution(mesh):
    fine = Mesh(mesh.devices.reshape(X, ZH, ZL, Y, C), ("x", "zh", "zl", "y", "c"))
    placed = (P(DP + ET, None), P(DP + ET), P(DP + ET), P(DP, ET), P(DP, ET), P(DP, ET))
    return jax.shard_map(
        shards, mesh=fine, in_specs=placed, out_specs=P(DP, ET), check_vma=False
    )
```

time: 536 us -> 125 us (0.23)
  the two profiles are of different devices: /device:TPU:6 before, /device:TPU:33 now
where the time goes in v1:
time: 125 us
  blocking collectives  53.1 us (42%)
  waiting for transfers between devices  29.8 us (24%)
  starting transfers between devices  17.6 us (14%)
  between operations  14.3 us (11%)
  other arithmetic  5.06 us (4%)
  matrix products  3.38 us (3%)
  local copies, waits for them, and re-layouts  1.35 us (1%)
    all_to_all x1, blocking collectives, shards(): arrived = lax.all_to_all(total.astype(jnp.bfloat16), 'zh', 0, 0)  33.1 us
    all_to_all x1, blocking collectives, shards(): own = lax.all_to_all(parts, ('x', 'y'), 0, 0)  19.9 us
    all_gather x1, waiting for transfers between devices, shards(): lax.all_gather(delta.reshape(C * Y * rows, units), 'x', axis=0, tiled=False)  15.3 us
    ppermute x4, starting transfers between devices, z_shift(): lax.ppermute(value, Z, [(i, (i + step) % (ZH * ZL)) for i in range(ZH * Z...  14 us
    ppermute x4, waiting for transfers between devices, z_shift(): lax.ppermute(value, Z, [(i, (i + step) % (ZH * ZL)) for i in range(ZH * Z...  12.7 us
    ppermute x1, starting transfers between devices, shards(): other = lax.ppermute(own, 'c', [(0, 1), (1, 0)])  3.62 us
    dot_general x1, matrix products, shards(): lax.dot_general(tokens.reshape(X * C * Y * rows, part), delta.reshape(X *...  3.38 us
  transfers between devices with their start and end apart: 6, of which 3 were waited for; matrix products, arithmetic and copies ran while one was open for 1% of the time, Pallas kernels for 0%

profile of v1, /device:TPU:33, one launch (start us, length us, event | category | flops | bytes accessed | tf_op | source)
XLA Modules:
  0.0 124.6 jit_solution(9060567783473555367)
XLA Ops:
  6.5 0.0 all-gather.2.cloned.1.call-start
  6.5 1.9 %fusion.6 = bf16[256,1024]{1,0:T(8,128)(2,1)S(1)} fusion(bf16[256,1024]{1,0:T(8,128)(2,1)} %param.9, bf16[256,1024]{1,0:T(8,128)(2,1)} %param.10, bf16[256,1024]{1,0:T(8,128)(2,1)} %param.11), kind=kLoop, calls=%fused_computation.9 | loop fusion | flops 3407872 | bytes 2097152 | tf_op jit(solution)/shard_map/convert_element_type | solution.py:18
  8.4 0.0 copy-start.2
  8.4 0.0 copy-start.1
  8.5 0.8 pad_maximum_fusion.1
  9.3 0.0 all-gather.2.cloned.1.call-update
  10.0 0.0 copy-done.2
  10.0 0.1 multiply_convert_fusion
  10.1 0.1 reshape.24
  10.3 0.1 broadcast_in_dim.2
  10.4 19.9 %all_to_all.10 = bf16[16,32,768]{2,1,0:T(8,128)(2,1)S(1)} all-to-all(bf16[16,32,768]{2,1,0:T(8,128)(2,1)S(1)} %bitcast.47), channel_id=1, replica_groups=mesh['x'=4,'zh'=4,'zl'=4,'y'=4,'c'=2] {'x','y'}, dimensions={0} | all-to-all | bytes 1572864 | tf_op jit(solution)/shard_map/all_to_all | solution.py:52
  30.3 3.6 %collective-permute-start = (bf16[16,32,768]{2,1,0:T(8,128)(2,1)S(1)}, bf16[16,32,768]{2,1,0:T(8,128)(2,1)S(1)}, u32[]{:S(2)}, u32[]{:S(2)}) collective-permute-start(bf16[16,32,768]{2,1,0:T(8,128)(2,1)S(1)} %all_to_all.10), channel_id=1, source_target_pairs={{0,1},{1,0},{2,3},{3,2},{4,5},{5,4},{6,7},{7,6},{8,9},{9,8},{10,11... | collective-permute-start | bytes 2359304 | tf_op jit(solution)/shard_map/ppermute | solution.py:53
  34.0 1.8 %collective-permute-done = bf16[16,32,768]{2,1,0:T(8,128)(2,1)S(1)} collective-permute-done((bf16[16,32,768]{2,1,0:T(8,128)(2,1)S(1)}, bf16[16,32,768]{2,1,0:T(8,128)(2,1)S(1)}, u32[]{:S(2)}, u32[]{:S(2)}) %collective-permute-start) | collective-permute-done | bytes 786464 | tf_op jit(solution)/shard_map/ppermute | solution.py:53
  35.8 0.1 pad_maximum_fusion
  35.9 0.1 copy.19
  36.1 0.8 copy.20
  36.8 15.3 %all-gather.2.cloned.1.call-done = bf16[4,256,1024]{2,1,0:T(8,128)(2,1)} async-done(((bf16[1,256,1024]{2,1,0:T(8,128)(2,1)}), bf16[4,256,1024]{2,1,0:T(8,128)(2,1)}) %all-gather.2.cloned.1.call-update) | async-done | bytes 2097168 | tf_op jit(solution)/shard_map/all_gather | solution.py:45
  52.1 3.4 %fusion.14 = f32[4,4,48,1024]{3,2,1,0:T(8,128)S(1)} fusion(bf16[4,4,48,1024]{3,2,1,0:T(8,128)(2,1)S(1)} %bitcast.50, bf16[1024,1024,1,1]{1,0,3,2:T(8,128)(2,1)} %bitcast.53), kind=kOutput, calls=%fused_computation.28 | convolution fusion | flops 1610612736 | bytes 6815744 | tf_op jit(solution)/shard_map/dot_general | solution.py:58
  55.5 0.2 fusion.10
  55.7 2.1 %collective-permute-start.2 = (bf16[4,48,1024]{2,1,0:T(8,128)(2,1)S(1)}, bf16[4,48,1024]{2,1,0:T(8,128)(2,1)S(1)}, u32[]{:S(2)}, u32[]{:S(2)}) collective-permute-start(bf16[4,48,1024]{2,1,0:T(8,128)(2,1)S(1)} %get-tuple-element.7), channel_id=1, source_target_pairs={{0,120},{8,0},{16,8},{24,16},{32,24},{40,32},{48,40},{56,48},{64,5... | collective-permute-start | bytes 1179656 | tf_op jit(solution)/shard_map/ppermute | solution.py:24
  57.8 3.2 %collective-permute-start.1 = (bf16[4,48,1024]{2,1,0:T(8,128)(2,1)S(1)}, bf16[4,48,1024]{2,1,0:T(8,128)(2,1)S(1)}, u32[]{:S(2)}, u32[]{:S(2)}) collective-permute-start(bf16[4,48,1024]{2,1,0:T(8,128)(2,1)S(1)} %get-tuple-element.6), channel_id=1, source_target_pairs={{0,8},{8,16},{16,24},{24,32},{32,40},{40,48},{48,56},{56,64},{64,7... | collective-permute-start | bytes 1179656 | tf_op jit(solution)/shard_map/ppermute | solution.py:24
  61.0 0.0 copy-done
  61.0 5.4 %collective-permute-start.4 = (bf16[4,48,512]{2,1,0:T(8,128)(2,1)S(1)}, bf16[4,48,512]{2,1,0:T(8,128)(2,1)S(1)}, u32[]{:S(2)}, u32[]{:S(2)}) collective-permute-start(bf16[4,48,512]{2,1,0:T(8,128)(2,1)S(1)} %get-tuple-element.11), channel_id=1, source_target_pairs={{0,16},{8,24},{16,32},{24,40},{32,48},{40,56},{48,64},{56,72},{64,... | collective-permute-start | bytes 589832 | tf_op jit(solution)/shard_map/ppermute | solution.py:24
  66.4 3.3 %collective-permute-start.3 = (bf16[4,48,512]{2,1,0:T(8,128)(2,1)S(1)}, bf16[4,48,512]{2,1,0:T(8,128)(2,1)S(1)}, u32[]{:S(2)}, u32[]{:S(2)}) collective-permute-start(bf16[4,48,512]{2,1,0:T(8,128)(2,1)S(1)} %get-tuple-element.10), channel_id=1, source_target_pairs={{0,112},{8,120},{16,0},{24,8},{32,16},{40,24},{48,32},{56,40},{64,... | collective-permute-start | bytes 589832 | tf_op jit(solution)/shard_map/ppermute | solution.py:24
  69.7 12.7 %collective-permute-done.4 = bf16[4,48,512]{2,1,0:T(8,128)(2,1)S(1)} collective-permute-done((bf16[4,48,512]{2,1,0:T(8,128)(2,1)S(1)}, bf16[4,48,512]{2,1,0:T(8,128)(2,1)S(1)}, u32[]{:S(2)}, u32[]{:S(2)}) %collective-permute-start.4) | collective-permute-done | bytes 196640 | tf_op jit(solution)/shard_map/ppermute | solution.py:24
  82.4 0.0 collective-permute-done.3
  82.4 0.0 collective-permute-done.2
  82.5 0.0 collective-permute-done.1
  82.5 1.4 %fusion.9 = bf16[4,48,1024]{2,1,0:T(8,128)(2,1)S(1)} fusion(bf16[4,48,1024]{2,1,0:T(8,128)(2,1)S(1)} %collective-permute-done.2, bf16[4,48,1024]{2,1,0:T(8,128)(2,1)S(1)} %collective-permute-done.1, f32[4,4,48,1024]{3,2,1,0:T(8,128)} %copy-done, s32[]{:T(128)S(6)} %select_n.37, bf16[4,48,512]{2,1,0:T(8,128)(2,1)S(1)} %collective-permute-done.4, ...), kind=kLoop, calls=%fused_computation.15 | loop fusion | flops 1966080 | bytes 2359300 | tf_op jit(solution)/shard_map/convert_element_type | solution.py:75
  83.8 33.1 %all_to_all.11 = bf16[4,48,1024]{2,1,0:T(8,128)(2,1)S(1)} all-to-all(bf16[4,48,1024]{2,1,0:T(8,128)(2,1)S(1)} %fusion.9), channel_id=1, replica_groups=mesh['x'=4,'zh'=4,'zl'=4,'y'=4,'c'=2] {'zh'}, dimensions={0} | all-to-all | bytes 786432 | tf_op jit(solution)/shard_map/all_to_all | solution.py:75
  117.0 0.1 convert_reduce_fusion
  117.0 0.7 broadcast_multiply_fusion
  (6 shorter events, 0.1 us)
Async XLA Ops:
  6.5 45.6 %all-gather.2.cloned.1.call-start = ((), (), s32[]{:S(2)}) async-start(), calls=%async_computation.2 | async-start | bytes 2621440 | tf_op jit(solution)/shard_map/all_gather | solution.py:45
  8.4 1.6 %copy-start.2 = (f32[32]{0:T(128)S(1)}, f32[32]{0:T(128)}, u32[]{:S(2)}) copy-start(f32[32]{0:T(128)} %param.7) | copy-start | bytes 388
  8.4 1.6 %copy-start.1 = (bf16[32,3072]{1,0:T(8,128)(2,1)S(1)}, bf16[32,3072]{1,0:T(8,128)(2,1)}, u32[]{:S(2)}) copy-start(bf16[32,3072]{1,0:T(8,128)(2,1)} %param.6) | copy-start | bytes 589828
  30.3 5.5 %collective-permute-start = (bf16[16,32,768]{2,1,0:T(8,128)(2,1)S(1)}, bf16[16,32,768]{2,1,0:T(8,128)(2,1)S(1)}, u32[]{:S(2)}, u32[]{:S(2)}) collective-permute-start(bf16[16,32,768]{2,1,0:T(8,128)(2,1)S(1)} %all_to_all.10), channel_id=1, source_target_pairs={{0,1},{1,0},{2,3},{3,2},{4,5},{5,4},{6,7},{7,6},{8,9},{9,8},{10,11... | collective-permute-start | bytes 2359304 | tf_op jit(solution)/shard_map/ppermute | solution.py:53
  55.5 5.5 %copy-start = (f32[4,4,48,1024]{3,2,1,0:T(8,128)}, f32[4,4,48,1024]{3,2,1,0:T(8,128)S(1)}, u32[]{:S(2)}) copy-start(f32[4,4,48,1024]{3,2,1,0:T(8,128)S(1)} %fusion.14) | copy-start | bytes 9437188
  55.7 26.8 %collective-permute-start.2 = (bf16[4,48,1024]{2,1,0:T(8,128)(2,1)S(1)}, bf16[4,48,1024]{2,1,0:T(8,128)(2,1)S(1)}, u32[]{:S(2)}, u32[]{:S(2)}) collective-permute-start(bf16[4,48,1024]{2,1,0:T(8,128)(2,1)S(1)} %get-tuple-element.7), channel_id=1, source_target_pairs={{0,120},{8,0},{16,8},{24,16},{32,24},{40,32},{48,40},{56,48},{64,5... | collective-permute-start | bytes 1179656 | tf_op jit(solution)/shard_map/ppermute | solution.py:24
  57.8 24.7 %collective-permute-start.1 = (bf16[4,48,1024]{2,1,0:T(8,128)(2,1)S(1)}, bf16[4,48,1024]{2,1,0:T(8,128)(2,1)S(1)}, u32[]{:S(2)}, u32[]{:S(2)}) collective-permute-start(bf16[4,48,1024]{2,1,0:T(8,128)(2,1)S(1)} %get-tuple-element.6), channel_id=1, source_target_pairs={{0,8},{8,16},{16,24},{24,32},{32,40},{40,48},{48,56},{56,64},{64,7... | collective-permute-start | bytes 1179656 | tf_op jit(solution)/shard_map/ppermute | solution.py:24
  61.0 21.4 %collective-permute-start.4 = (bf16[4,48,512]{2,1,0:T(8,128)(2,1)S(1)}, bf16[4,48,512]{2,1,0:T(8,128)(2,1)S(1)}, u32[]{:S(2)}, u32[]{:S(2)}) collective-permute-start(bf16[4,48,512]{2,1,0:T(8,128)(2,1)S(1)} %get-tuple-element.11), channel_id=1, source_target_pairs={{0,16},{8,24},{16,32},{24,40},{32,48},{40,56},{48,64},{56,72},{64,... | collective-permute-start | bytes 589832 | tf_op jit(solution)/shard_map/ppermute | solution.py:24
  66.4 16.1 %collective-permute-start.3 = (bf16[4,48,512]{2,1,0:T(8,128)(2,1)S(1)}, bf16[4,48,512]{2,1,0:T(8,128)(2,1)S(1)}, u32[]{:S(2)}, u32[]{:S(2)}) collective-permute-start(bf16[4,48,512]{2,1,0:T(8,128)(2,1)S(1)} %get-tuple-element.10), channel_id=1, source_target_pairs={{0,112},{8,120},{16,0},{24,8},{32,16},{40,24},{48,32},{56,40},{64,... | collective-permute-start | bytes 589832 | tf_op jit(solution)/shard_map/ppermute | solution.py:24
Sparse Core Ops, SparseCore 0:
  9.5 42.5 all-gather.1

commit v2 on v1

v2 whole, which is shorter than its diff:
```python
import functools
import math

import jax
import jax.numpy as jnp
from jax import lax
from jax.experimental import pallas as pl
from jax.experimental.pallas import tpu as pltpu
from jax.sharding import Mesh, PartitionSpec as P

X, Z, Y, C = 4, 16, 4, 2
W = 4
DP = ("x", "z")
ET = ("y", "c")
VMEM = pl.BlockSpec(memory_space=pltpu.VMEM)
SMEM = pl.BlockSpec(memory_space=pltpu.SMEM)
PARAMS = pltpu.CompilerParams(vmem_limit_bytes=11 * 512 * 1024)


def f32(value):
    return value.astype(jnp.float32)


def bf16(value):
    return value.astype(jnp.bfloat16)


def x_shift(value, step):
    return lax.ppermute(value, "x", [(i, (i + step) % X) for i in range(X)])


def x_forward(value):
    pairs = [(x * C + c, (x + 1 - 2 * c) % X * C + c) for x in range(X) for c in range(C)]
    return lax.ppermute(value, ("x", "c"), pairs)


def z_shift(value, step):
    return lax.ppermute(value, "z", [(i, (i + step) % Z) for i in range(Z)])


def z_apart(value, step):
    pairs = [(z * C + c, (z - step + 2 * step * c) % Z * C + c) for z in range(Z) for c in range(C)]
    return lax.ppermute(value, ("z", "c"), pairs)


def delta_kernel(at, gate_ref, up_ref, grad_ref, out_ref):
    rows = gate_ref.shape[2]
    for place in range(C):
        source = (at[0] + place) % C
        for y in range(Y):
            gate = f32(gate_ref[y, source])
            sigmoid_v = jax.nn.sigmoid(gate)
            slope = sigmoid_v * (1.0 + gate * (1.0 - sigmoid_v))
            value = f32(grad_ref[y, source]) * f32(up_ref[y, source]) * slope
            out_ref[(place * Y + y) * rows : (place * Y + y + 1) * rows, :] = bf16(value)


def slab_kernel(at, total_ref, keep_ref, *sent_refs):
    for j in range(Z // W):
        keep_ref[j] = total_ref[j * W + at[0]]
        for step, sent_ref in enumerate(sent_refs):
            sent_ref[j] = bf16(total_ref[j * W + (at[0] + step + 1) % W])


def window_kernel(at, keep_ref, far_ref, above_ref, below_ref, own_ref, *sent_refs):
    for step, out_ref in enumerate((own_ref,) + sent_refs):
        j = (at[0] + step) % (Z // W)
        value = keep_ref[j] + f32(far_ref[j]) + f32(above_ref[j]) + f32(below_ref[j])
        out_ref[...] = value.astype(out_ref.dtype)


def shards(token_rows, route_weight, live_count, gate_pre, up_pre, hidden_grad):
    rows, features = token_rows.shape
    units = gate_pre.shape[1]
    part = features // X
    owned = part // Z
    core = lax.axis_index("c")
    x_at = lax.axis_index("x")
    z_at = lax.axis_index("z")
    shape = jax.ShapeDtypeStruct

    live_rows = jnp.arange(rows, dtype=jnp.int32) < live_count[0]
    factor = route_weight * f32(live_rows)
    weighted = bf16(f32(token_rows) * factor[:, None])
    weighted = jnp.broadcast_to(weighted[None], (Y, rows, features))
    by_core = [value.reshape(Y, C, rows, units) for value in (gate_pre, up_pre, hidden_grad)]
    tall = Y * C * rows
    chunk = 256
    piece = pl.BlockSpec((Y, C, rows, chunk), lambda n, at: (0, 0, 0, n))
    delta = pl.pallas_call(
        delta_kernel,
        out_shape=shape((tall, units), jnp.bfloat16),
        grid_spec=pltpu.PrefetchScalarGridSpec(
            num_scalar_prefetch=1,
            grid=(units // chunk,),
            in_specs=[piece] * 3,
            out_specs=pl.BlockSpec((tall, chunk), lambda n, at: (0, n)),
        ),
        compiler_params=PARAMS,
        name="gate_delta",
    )(jnp.stack([core]), *by_core)

    along_y = lax.all_to_all(weighted, "y", 0, 0)
    parts = along_y.reshape(Y * rows, X, part).transpose(1, 0, 2)
    before, after = x_shift(delta, 1), x_shift(delta, -1)
    across = x_forward(jnp.where(core == 0, before, after))
    own = lax.all_to_all(parts, "x", 0, 0)
    own = jnp.stack(
        [
            lax.dynamic_index_in_dim(own, (x_at + step) % X, 0, keepdims=False)
            for step in (0, X - 1, 1, 2)
        ]
    )
    own, across = lax.optimization_barrier((own, across))
    other = lax.ppermute(own, "c", [(0, 1), (1, 0)])
    product = 0.0
    for place, tokens in enumerate((own, other)):
        span = slice(place * Y * rows, (place + 1) * Y * rows)
        right = jnp.concatenate([block[span] for block in (delta, before, after, across)], axis=0)
        product += lax.dot_general(
            tokens.reshape(X * Y * rows, part),
            right,
            (((0,), (0,)), ((), ())),
            preferred_element_type=jnp.float32,
        )

    count = Z // W
    keep, above, across_rows, below = pl.pallas_call(
        slab_kernel,
        out_shape=[shape((count, owned, units), jnp.float32)]
        + [shape((count, owned, units), jnp.bfloat16)] * (W - 1),
        in_specs=[SMEM, VMEM],
        out_specs=[VMEM] * W,
        compiler_params=PARAMS,
        name="slabs",
    )(jnp.stack([z_at % W]), product.reshape(Z, owned, units))

    far = z_apart(across_rows, 2)
    above = z_shift(above, 1)
    below = z_shift(below, -1)
    own_block, *blocks = pl.pallas_call(
        window_kernel,
        out_shape=[shape((owned, units), jnp.float32)]
        + [shape((owned, units), jnp.bfloat16)] * (count - 1),
        in_specs=[SMEM] + [VMEM] * 4,
        out_specs=[VMEM] * count,
        compiler_params=PARAMS,
        name="window",
    )(jnp.stack([z_at // W]), keep, far, above, below)

    total = own_block
    for step in (2, 1, 3):
        total += f32(z_shift(blocks[step - 1], W * step))
    return total * (1.0 / math.sqrt(rows * X * Z * Y * C))


def solution(mesh):
    fine = Mesh(mesh.devices.reshape(X, Z, Y, C), ("x", "z", "y", "c"))
    placed = (P(DP + ET, None), P(DP + ET), P(DP + ET), P(DP, ET), P(DP, ET), P(DP, ET))
    return jax.shard_map(
        shards, mesh=fine, in_specs=placed, out_specs=P(DP, ET), check_vma=False
    )
```

time: 125 us -> 112 us (0.90)
  the two profiles are of different devices: /device:TPU:33 before, /device:TPU:1 now
where the time goes in v2:
time: 112 us; the launch traced here: 111 us
  starting transfers between devices  60.4 us (54%)
  waiting for transfers between devices  38.2 us (34%)
  local copies, waits for them, and re-layouts  3.74 us (3%)
  other arithmetic  3.37 us (3%)
  matrix products  3.16 us (3%)
  Pallas kernels  1.12 us (1%)
    ppermute x5, starting transfers between devices, z_shift(): return lax.ppermute(value, 'z', [(i, (i + step) % Z) for i in range(Z)])  28.6 us
    ppermute x5, waiting for transfers between devices, z_shift(): return lax.ppermute(value, 'z', [(i, (i + step) % Z) for i in range(Z)])  21.3 us
    ppermute x1, waiting for transfers between devices, x_forward(): return lax.ppermute(value, ('x', 'c'), pairs)  7.81 us
    all_to_all x1, starting transfers between devices, shards(): own = lax.all_to_all(parts, 'x', 0, 0)  7.05 us
    ppermute x2, starting transfers between devices, x_shift(): return lax.ppermute(value, 'x', [(i, (i + step) % X) for i in range(X)])  6.49 us
    ppermute x1, starting transfers between devices, shards(): other = lax.ppermute(own, 'c', [(0, 1), (1, 0)])  5.18 us
    all_to_all x1, starting transfers between devices, shards(): along_y = lax.all_to_all(weighted, 'y', 0, 0)  5.01 us
    ppermute x1, starting transfers between devices, x_forward(): return lax.ppermute(value, ('x', 'c'), pairs)  4.57 us
  transfers between devices with their start and end apart: 12, of which 8 were waited for; matrix products, arithmetic and copies ran while one was open for 3% of the time, Pallas kernels for 1%

profile of v2, /device:TPU:1, one launch (start us, length us, event | category | flops | bytes accessed | tf_op | source)
XLA Modules:
  0.0 111.0 jit_solution(145563051835482874)
XLA Ops:
  0.8 0.7 compare_select_fusion
  1.4 1.0 multiply_convert_fusion
  2.5 1.0 broadcast_in_dim.2
  3.4 5.0 %all-to-all-start = ((bf16[4,32,3072]{2,1,0:T(8,128)(2,1)}), bf16[4,32,3072]{2,1,0:T(8,128)(2,1)S(1)}, u32[]{:S(2)}, u32[]{:S(2)}) async-start(bf16[4,32,3072]{2,1,0:T(8,128)(2,1)} %broadcast_in_dim.2), calls=%async_computation | async-start | bytes 1572864 | tf_op jit(solution)/shard_map/all_to_all | solution.py:103
  8.5 0.8 gate_delta.1
  9.2 3.1 %collective-permute-start = (bf16[256,1024]{1,0:T(8,128)(2,1)S(1)}, bf16[256,1024]{1,0:T(8,128)(2,1)S(1)}, u32[]{:S(2)}, u32[]{:S(2)}) collective-permute-start(bf16[256,1024]{1,0:T(8,128)(2,1)S(1)} %gate_delta.1), channel_id=1, source_target_pairs={{0,128},{128,256},{256,384},{384,0},{1,129},{129,257},{257,385},{3... | collective-permute-start | bytes 1572872 | tf_op jit(solution)/shard_map/ppermute | solution.py:29
  12.4 3.4 %collective-permute-start.1 = (bf16[256,1024]{1,0:T(8,128)(2,1)S(1)}, bf16[256,1024]{1,0:T(8,128)(2,1)S(1)}, u32[]{:S(2)}, u32[]{:S(2)}) collective-permute-start(bf16[256,1024]{1,0:T(8,128)(2,1)S(1)} %gate_delta.1), channel_id=1, source_target_pairs={{0,384},{128,0},{256,128},{384,256},{1,385},{129,1},{257,129},{385... | collective-permute-start | bytes 1572872 | tf_op jit(solution)/shard_map/ppermute | solution.py:29
  15.8 1.0 all-to-all-done
  16.8 0.6 reshape.23
  17.4 1.0 copy.9
  18.3 7.0 %all-to-all-start.1 = ((bf16[4,128,768]{2,1,0:T(8,128)(2,1)}), bf16[4,128,768]{2,1,0:T(8,128)(2,1)S(1)}, u32[]{:S(2)}, u32[]{:S(2)}) async-start(bf16[4,128,768]{2,1,0:T(8,128)(2,1)} %copy.9), calls=%async_computation.1 | async-start | bytes 1572864 | tf_op jit(solution)/shard_map/all_to_all | solution.py:107
  25.4 0.9 broadcast_select_fusion
  26.2 4.6 %collective-permute-start.2 = (bf16[256,1024]{1,0:T(8,128)(2,1)}, bf16[256,1024]{1,0:T(8,128)(2,1)}, u32[]{:S(2)}, u32[]{:S(2)}) collective-permute-start(bf16[256,1024]{1,0:T(8,128)(2,1)} %broadcast_select_fusion), channel_id=1, source_target_pairs={{0,128},{1,385},{128,256},{129,1},{256,384},{257,129},{384,0},{385... | collective-permute-start | bytes 1572872 | tf_op jit(solution)/shard_map/ppermute | solution.py:34
  30.9 3.6 %all-to-all-done.1 = bf16[4,128,768]{2,1,0:T(8,128)(2,1)S(1)} async-done(((bf16[4,128,768]{2,1,0:T(8,128)(2,1)}), bf16[4,128,768]{2,1,0:T(8,128)(2,1)S(1)}, u32[]{:S(2)}, u32[]{:S(2)}) %all-to-all-start.1) | async-done | bytes 786464 | tf_op jit(solution)/shard_map/all_to_all | solution.py:107
  34.7 7.8 %collective-permute-done.2 = bf16[256,1024]{1,0:T(8,128)(2,1)} collective-permute-done((bf16[256,1024]{1,0:T(8,128)(2,1)}, bf16[256,1024]{1,0:T(8,128)(2,1)}, u32[]{:S(2)}, u32[]{:S(2)}) %collective-permute-start.2) | collective-permute-done | bytes 524320 | tf_op jit(solution)/shard_map/ppermute | solution.py:34
  42.5 5.2 %collective-permute-start.3 = (bf16[4,128,768]{2,1,0:T(8,128)(2,1)S(1)}, bf16[4,128,768]{2,1,0:T(8,128)(2,1)}, u32[]{:S(2)}, u32[]{:S(2)}) collective-permute-start(bf16[4,128,768]{2,1,0:T(8,128)(2,1)S(1)} %pad_maximum_fusion), channel_id=1, source_target_pairs={{0,1},{1,0},{2,3},{3,2},{4,5},{5,4},{6,7},{7,6},{8,9},{9,8},{10,11... | collective-permute-start | bytes 2359304 | tf_op jit(solution)/shard_map/ppermute | solution.py:115
  47.8 1.1 fusion.20
  48.9 0.8 collective-permute-done.3
  49.7 2.1 %fusion.7 = f32[768,1024]{1,0:T(8,128)S(1)} fusion(bf16[512,768]{1,0:T(8,128)(2,1)} %bitcast.9, bf16[128,1024]{1,0:T(8,128)(2,1)S(1)} %get-tuple-element.36, bf16[128,1024]{1,0:T(8,128)(2,1)S(1)} %get-tuple-element.34, bf16[128,1024]{1,0:T(8,128)(2,1)S(1)} %get-tuple-element.32, bf16[128,1024]{1,0:T(8,128)(2,1)S(1)} %get-tuple-element.30), kind=kOutput, calls=%fused_computation.8 | convolution fusion | flops 809500672 | bytes 4980736 | tf_op jit(solution)/shard_map/dot_general | solution.py:120
  51.8 1.0 convolution_add_fusion
  52.9 0.2 slabs.1
  53.0 3.5 %collective-permute-start.4 = (bf16[4,48,1024]{2,1,0:T(8,128)(2,1)S(1)}, bf16[4,48,1024]{2,1,0:T(8,128)(2,1)S(1)}, u32[]{:S(2)}, u32[]{:S(2)}) collective-permute-start(bf16[4,48,1024]{2,1,0:T(8,128)(2,1)S(1)} %get-tuple-element.18), channel_id=1, source_target_pairs={{0,112},{1,17},{8,120},{9,25},{16,0},{17,33},{24,8},{25,41},{32,16... | collective-permute-start | bytes 1179656 | tf_op jit(solution)/shard_map/ppermute | solution.py:43
  56.5 3.5 %collective-permute-start.5 = (bf16[4,48,1024]{2,1,0:T(8,128)(2,1)S(1)}, bf16[4,48,1024]{2,1,0:T(8,128)(2,1)S(1)}, u32[]{:S(2)}, u32[]{:S(2)}) collective-permute-start(bf16[4,48,1024]{2,1,0:T(8,128)(2,1)S(1)} %get-tuple-element.19), channel_id=1, source_target_pairs={{0,8},{8,16},{16,24},{24,32},{32,40},{40,48},{48,56},{56,64},{64,7... | collective-permute-start | bytes 1179656 | tf_op jit(solution)/shard_map/ppermute | solution.py:38
  60.1 6.5 %collective-permute-start.6 = (bf16[4,48,1024]{2,1,0:T(8,128)(2,1)S(1)}, bf16[4,48,1024]{2,1,0:T(8,128)(2,1)S(1)}, u32[]{:S(2)}, u32[]{:S(2)}) collective-permute-start(bf16[4,48,1024]{2,1,0:T(8,128)(2,1)S(1)} %get-tuple-element.20), channel_id=1, source_target_pairs={{0,120},{8,0},{16,8},{24,16},{32,24},{40,32},{48,40},{56,48},{64,5... | collective-permute-start | bytes 1179656 | tf_op jit(solution)/shard_map/ppermute | solution.py:38
  66.6 3.7 %collective-permute-done.4.far_ref = bf16[4,48,1024]{2,1,0:T(8,128)(2,1)S(1)} collective-permute-done((bf16[4,48,1024]{2,1,0:T(8,128)(2,1)S(1)}, bf16[4,48,1024]{2,1,0:T(8,128)(2,1)S(1)}, u32[]{:S(2)}, u32[]{:S(2)}) %collective-permute-start.4) | collective-permute-done | bytes 393248 | tf_op jit(solution)/shard_map/ppermute | solution.py:43
  70.3 10.3 %collective-permute-done.5.above_ref = bf16[4,48,1024]{2,1,0:T(8,128)(2,1)S(1)} collective-permute-done((bf16[4,48,1024]{2,1,0:T(8,128)(2,1)S(1)}, bf16[4,48,1024]{2,1,0:T(8,128)(2,1)S(1)}, u32[]{:S(2)}, u32[]{:S(2)}) %collective-permute-start.5) | collective-permute-done | bytes 393248 | tf_op jit(solution)/shard_map/ppermute | solution.py:38
  80.7 9.3 %collective-permute-start.7 = (bf16[48,1024]{1,0:T(8,128)(2,1)S(1)}, bf16[48,1024]{1,0:T(8,128)(2,1)S(1)}, u32[]{:S(2)}, u32[]{:S(2)}) collective-permute-start(bf16[48,1024]{1,0:T(8,128)(2,1)S(1)} %get-tuple-element.22), channel_id=1, source_target_pairs={{0,64},{8,72},{16,80},{24,88},{32,96},{40,104},{48,112},{56,120},{... | collective-permute-start | bytes 294920 | tf_op jit(solution)/shard_map/ppermute | solution.py:38
  90.1 4.0 %collective-permute-start.8 = (bf16[48,1024]{1,0:T(8,128)(2,1)S(1)}, bf16[48,1024]{1,0:T(8,128)(2,1)S(1)}, u32[]{:S(2)}, u32[]{:S(2)}) collective-permute-start(bf16[48,1024]{1,0:T(8,128)(2,1)S(1)} %get-tuple-element.23), channel_id=1, source_target_pairs={{0,32},{8,40},{16,48},{24,56},{32,64},{40,72},{48,80},{56,88},{64,... | collective-permute-start | bytes 294920 | tf_op jit(solution)/shard_map/ppermute | solution.py:38
  94.1 5.2 %collective-permute-start.9 = (bf16[48,1024]{1,0:T(8,128)(2,1)S(1)}, bf16[48,1024]{1,0:T(8,128)(2,1)S(1)}, u32[]{:S(2)}, u32[]{:S(2)}) collective-permute-start(bf16[48,1024]{1,0:T(8,128)(2,1)S(1)} %get-tuple-element.24), channel_id=1, source_target_pairs={{0,96},{8,104},{16,112},{24,120},{32,0},{40,8},{48,16},{56,24},{64... | collective-permute-start | bytes 294920 | tf_op jit(solution)/shard_map/ppermute | solution.py:38
  99.3 3.2 %collective-permute-done.8 = bf16[48,1024]{1,0:T(8,128)(2,1)S(1)} collective-permute-done((bf16[48,1024]{1,0:T(8,128)(2,1)S(1)}, bf16[48,1024]{1,0:T(8,128)(2,1)S(1)}, u32[]{:S(2)}, u32[]{:S(2)}) %collective-permute-start.8) | collective-permute-done | bytes 98336 | tf_op jit(solution)/shard_map/ppermute | solution.py:38
  102.4 7.8 %collective-permute-done.9 = bf16[48,1024]{1,0:T(8,128)(2,1)S(1)} collective-permute-done((bf16[48,1024]{1,0:T(8,128)(2,1)S(1)}, bf16[48,1024]{1,0:T(8,128)(2,1)S(1)}, u32[]{:S(2)}, u32[]{:S(2)}) %collective-permute-start.9) | collective-permute-done | bytes 98336 | tf_op jit(solution)/shard_map/ppermute | solution.py:38
  110.3 0.7 add_multiply_fusion
  (16 shorter events, 0.5 us)
Async XLA Ops:
  0.0 8.4 %copy-start = (bf16[256,1024]{1,0:T(8,128)(2,1)S(1)}, bf16[256,1024]{1,0:T(8,128)(2,1)}, u32[]{:S(2)}) copy-start(bf16[256,1024]{1,0:T(8,128)(2,1)} %param.9) | copy-start | bytes 1572868
  0.0 8.4 %copy-start.1 = (bf16[256,1024]{1,0:T(8,128)(2,1)S(1)}, bf16[256,1024]{1,0:T(8,128)(2,1)}, u32[]{:S(2)}) copy-start(bf16[256,1024]{1,0:T(8,128)(2,1)} %param.10) | copy-start | bytes 1572868
  0.0 8.4 %copy-start.2 = (bf16[256,1024]{1,0:T(8,128)(2,1)S(1)}, bf16[256,1024]{1,0:T(8,128)(2,1)}, u32[]{:S(2)}) copy-start(bf16[256,1024]{1,0:T(8,128)(2,1)} %param.11) | copy-start | bytes 1572868
  3.4 13.4 %all-to-all-start = ((bf16[4,32,3072]{2,1,0:T(8,128)(2,1)}), bf16[4,32,3072]{2,1,0:T(8,128)(2,1)S(1)}, u32[]{:S(2)}, u32[]{:S(2)}) async-start(bf16[4,32,3072]{2,1,0:T(8,128)(2,1)} %broadcast_in_dim.2), calls=%async_computation | async-start | bytes 1572864 | tf_op jit(solution)/shard_map/all_to_all | solution.py:103
  9.2 16.1 %collective-permute-start = (bf16[256,1024]{1,0:T(8,128)(2,1)S(1)}, bf16[256,1024]{1,0:T(8,128)(2,1)S(1)}, u32[]{:S(2)}, u32[]{:S(2)}) collective-permute-start(bf16[256,1024]{1,0:T(8,128)(2,1)S(1)} %gate_delta.1), channel_id=1, source_target_pairs={{0,128},{128,256},{256,384},{384,0},{1,129},{129,257},{257,385},{3... | collective-permute-start | bytes 1572872 | tf_op jit(solution)/shard_map/ppermute | solution.py:29
  12.4 13.0 %collective-permute-start.1 = (bf16[256,1024]{1,0:T(8,128)(2,1)S(1)}, bf16[256,1024]{1,0:T(8,128)(2,1)S(1)}, u32[]{:S(2)}, u32[]{:S(2)}) collective-permute-start(bf16[256,1024]{1,0:T(8,128)(2,1)S(1)} %gate_delta.1), channel_id=1, source_target_pairs={{0,384},{128,0},{256,128},{384,256},{1,385},{129,1},{257,129},{385... | collective-permute-start | bytes 1572872 | tf_op jit(solution)/shard_map/ppermute | solution.py:29
  18.3 16.2 %all-to-all-start.1 = ((bf16[4,128,768]{2,1,0:T(8,128)(2,1)}), bf16[4,128,768]{2,1,0:T(8,128)(2,1)S(1)}, u32[]{:S(2)}, u32[]{:S(2)}) async-start(bf16[4,128,768]{2,1,0:T(8,128)(2,1)} %copy.9), calls=%async_computation.1 | async-start | bytes 1572864 | tf_op jit(solution)/shard_map/all_to_all | solution.py:107
  26.2 16.2 %collective-permute-start.2 = (bf16[256,1024]{1,0:T(8,128)(2,1)}, bf16[256,1024]{1,0:T(8,128)(2,1)}, u32[]{:S(2)}, u32[]{:S(2)}) collective-permute-start(bf16[256,1024]{1,0:T(8,128)(2,1)} %broadcast_select_fusion), channel_id=1, source_target_pairs={{0,128},{1,385},{128,256},{129,1},{256,384},{257,129},{384,0},{385... | collective-permute-start | bytes 1572872 | tf_op jit(solution)/shard_map/ppermute | solution.py:34
  42.5 7.2 %collective-permute-start.3 = (bf16[4,128,768]{2,1,0:T(8,128)(2,1)S(1)}, bf16[4,128,768]{2,1,0:T(8,128)(2,1)}, u32[]{:S(2)}, u32[]{:S(2)}) collective-permute-start(bf16[4,128,768]{2,1,0:T(8,128)(2,1)S(1)} %pad_maximum_fusion), channel_id=1, source_target_pairs={{0,1},{1,0},{2,3},{3,2},{4,5},{5,4},{6,7},{7,6},{8,9},{9,8},{10,11... | collective-permute-start | bytes 2359304 | tf_op jit(solution)/shard_map/ppermute | solution.py:115
  53.0 17.2 %collective-permute-start.4 = (bf16[4,48,1024]{2,1,0:T(8,128)(2,1)S(1)}, bf16[4,48,1024]{2,1,0:T(8,128)(2,1)S(1)}, u32[]{:S(2)}, u32[]{:S(2)}) collective-permute-start(bf16[4,48,1024]{2,1,0:T(8,128)(2,1)S(1)} %get-tuple-element.18), channel_id=1, source_target_pairs={{0,112},{1,17},{8,120},{9,25},{16,0},{17,33},{24,8},{25,41},{32,16... | collective-permute-start | bytes 1179656 | tf_op jit(solution)/shard_map/ppermute | solution.py:43
  56.5 24.0 %collective-permute-start.5 = (bf16[4,48,1024]{2,1,0:T(8,128)(2,1)S(1)}, bf16[4,48,1024]{2,1,0:T(8,128)(2,1)S(1)}, u32[]{:S(2)}, u32[]{:S(2)}) collective-permute-start(bf16[4,48,1024]{2,1,0:T(8,128)(2,1)S(1)} %get-tuple-element.19), channel_id=1, source_target_pairs={{0,8},{8,16},{16,24},{24,32},{32,40},{40,48},{48,56},{56,64},{64,7... | collective-permute-start | bytes 1179656 | tf_op jit(solution)/shard_map/ppermute | solution.py:38
  60.1 20.5 %collective-permute-start.6 = (bf16[4,48,1024]{2,1,0:T(8,128)(2,1)S(1)}, bf16[4,48,1024]{2,1,0:T(8,128)(2,1)S(1)}, u32[]{:S(2)}, u32[]{:S(2)}) collective-permute-start(bf16[4,48,1024]{2,1,0:T(8,128)(2,1)S(1)} %get-tuple-element.20), channel_id=1, source_target_pairs={{0,120},{8,0},{16,8},{24,16},{32,24},{40,32},{48,40},{56,48},{64,5... | collective-permute-start | bytes 1179656 | tf_op jit(solution)/shard_map/ppermute | solution.py:38
  80.7 18.6 %collective-permute-start.7 = (bf16[48,1024]{1,0:T(8,128)(2,1)S(1)}, bf16[48,1024]{1,0:T(8,128)(2,1)S(1)}, u32[]{:S(2)}, u32[]{:S(2)}) collective-permute-start(bf16[48,1024]{1,0:T(8,128)(2,1)S(1)} %get-tuple-element.22), channel_id=1, source_target_pairs={{0,64},{8,72},{16,80},{24,88},{32,96},{40,104},{48,112},{56,120},{... | collective-permute-start | bytes 294920 | tf_op jit(solution)/shard_map/ppermute | solution.py:38
  90.1 12.4 %collective-permute-start.8 = (bf16[48,1024]{1,0:T(8,128)(2,1)S(1)}, bf16[48,1024]{1,0:T(8,128)(2,1)S(1)}, u32[]{:S(2)}, u32[]{:S(2)}) collective-permute-start(bf16[48,1024]{1,0:T(8,128)(2,1)S(1)} %get-tuple-element.23), channel_id=1, source_target_pairs={{0,32},{8,40},{16,48},{24,56},{32,64},{40,72},{48,80},{56,88},{64,... | collective-permute-start | bytes 294920 | tf_op jit(solution)/shard_map/ppermute | solution.py:38
  94.1 16.2 %collective-permute-start.9 = (bf16[48,1024]{1,0:T(8,128)(2,1)S(1)}, bf16[48,1024]{1,0:T(8,128)(2,1)S(1)}, u32[]{:S(2)}, u32[]{:S(2)}) collective-permute-start(bf16[48,1024]{1,0:T(8,128)(2,1)S(1)} %get-tuple-element.24), channel_id=1, source_target_pairs={{0,96},{8,104},{16,112},{24,120},{32,0},{40,8},{48,16},{56,24},{64... | collective-permute-start | bytes 294920 | tf_op jit(solution)/shard_map/ppermute | solution.py:38

commit v3 on v2

--- a/solution.py
+++ b/solution.py
@@ -55,6 +55,29 @@
             out_ref[(place * Y + y) * rows : (place * Y + y + 1) * rows, :] = bf16(value)
 
 
+def spread_kernel(rows_ref, out_ref):
+    for place in range(Y):
+        out_ref[place] = rows_ref[...]
+
+
+def choose_kernel(at, before_ref, after_ref, out_ref):
+    @pl.when(at[0] == 0)
+    def _():
+        out_ref[...] = before_ref[...]
+
+    @pl.when(at[0] != 0)
+    def _():
+        out_ref[...] = after_ref[...]
+
+
+def order_kernel(at, rows_ref, out_ref):
+    rows = rows_ref.shape[2]
+    for place in range(X):
+        for y in range(Y):
+            start = (place * Y + y) * rows
+            out_ref[start : start + rows, :] = rows_ref[y, at[place]]
+
+
 def slab_kernel(at, total_ref, keep_ref, *sent_refs):
     for j in range(Z // W):
         keep_ref[j] = total_ref[j * W + at[0]]
@@ -82,7 +105,6 @@
     live_rows = jnp.arange(rows, dtype=jnp.int32) < live_count[0]
     factor = route_weight * f32(live_rows)
     weighted = bf16(f32(token_rows) * factor[:, None])
-    weighted = jnp.broadcast_to(weighted[None], (Y, rows, features))
     by_core = [value.reshape(Y, C, rows, units) for value in (gate_pre, up_pre, hidden_grad)]
     tall = Y * C * rows
     chunk = 256
@@ -100,26 +122,48 @@
         name="gate_delta",
     )(jnp.stack([core]), *by_core)
 
-    along_y = lax.all_to_all(weighted, "y", 0, 0)
-    parts = along_y.reshape(Y * rows, X, part).transpose(1, 0, 2)
+    half = Y * rows
+    parts = lax.all_to_all(weighted.reshape(rows, X, part).transpose(1, 0, 2), "x", 0, 0)
+    parts, delta = lax.optimization_barrier((parts, delta))
     before, after = x_shift(delta, 1), x_shift(delta, -1)
-    across = x_forward(jnp.where(core == 0, before, after))
-    own = lax.all_to_all(parts, "x", 0, 0)
-    own = jnp.stack(
-        [
-            lax.dynamic_index_in_dim(own, (x_at + step) % X, 0, keepdims=False)
-            for step in (0, X - 1, 1, 2)
-        ]
-    )
-    own, across = lax.optimization_barrier((own, across))
+    chosen = pl.pallas_call(
+        choose_kernel,
+        out_shape=shape(delta.shape, delta.dtype),
+        in_specs=[SMEM, VMEM, VMEM],
+        out_specs=VMEM,
+        compiler_params=PARAMS,
+        cost_estimate=pl.CostEstimate(flops=int(2.3e+10), bytes_accessed=0, transcendentals=0),
+        name="chosen",
+    )(jnp.stack([core]), before, after)
+    across = x_forward(chosen)
+    spread = pl.pallas_call(
+        spread_kernel,
+        out_shape=shape((Y, X, rows, part), jnp.bfloat16),
+        in_specs=[VMEM],
+        out_specs=VMEM,
+        compiler_params=PARAMS,
+        cost_estimate=pl.CostEstimate(flops=int(2.3e+10), bytes_accessed=0, transcendentals=0),
+        name="spread",
+    )(parts)
+    own = lax.all_to_all(spread, "y", 0, 0)
+
+    own = pl.pallas_call(
+        order_kernel,
+        out_shape=shape((X * half, part), jnp.bfloat16),
+        in_specs=[SMEM, VMEM],
+        out_specs=VMEM,
+        compiler_params=PARAMS,
+        cost_estimate=pl.CostEstimate(flops=int(2.3e+10), bytes_accessed=0, transcendentals=0),
+        name="ordered_rows",
+    )((x_at + jnp.array([0, X - 1, 1, 2])) % X, own)
     other = lax.ppermute(own, "c", [(0, 1), (1, 0)])
     product = 0.0
     for place, tokens in enumerate((own, other)):
-        span = slice(place * Y * rows, (place + 1) * Y * rows)
-        right = jnp.concatenate([block[span] for block in (delta, before, after, across)], axis=0)
+        span = slice(place * half, (place + 1) * half)
+        right = [block[span] for block in (delta, before, after, across)]
         product += lax.dot_general(
-            tokens.reshape(X * Y * rows, part),
-            right,
+            tokens,
+            jnp.concatenate(right, axis=0),
             (((0,), (0,)), ((), ())),
             preferred_element_type=jnp.float32,
         )

time: 112 us -> 104 us (0.929)
  the two profiles are of different devices: /device:TPU:1 before, /device:TPU:8 now
where the time goes in v3:
time: 104 us
  starting transfers between devices  60.6 us (58%)
  waiting for transfers between devices  31 us (30%)
  local copies, waits for them, and re-layouts  3.96 us (4%)
  Pallas kernels  2.68 us (3%)
  other arithmetic  2.43 us (2%)
  matrix products  2.05 us (2%)
    ppermute x5, starting transfers between devices, z_shift(): return lax.ppermute(value, 'z', [(i, (i + step) % Z) for i in range(Z)])  26.5 us
    ppermute x5, waiting for transfers between devices, z_shift(): return lax.ppermute(value, 'z', [(i, (i + step) % Z) for i in range(Z)])  12.6 us
    ppermute x1, starting transfers between devices, z_apart(): return lax.ppermute(value, ('z', 'c'), pairs)  11.8 us
    all_to_all x1, starting transfers between devices, shards(): own = lax.all_to_all(spread, 'y', 0, 0)  8.33 us
    ppermute x2, starting transfers between devices, x_shift(): return lax.ppermute(value, 'x', [(i, (i + step) % X) for i in range(X)])  5.83 us
    ppermute x1, waiting for transfers between devices, x_forward(): return lax.ppermute(value, ('x', 'c'), pairs)  5.21 us
    ppermute x1, waiting for transfers between devices, z_apart(): return lax.ppermute(value, ('z', 'c'), pairs)  4.75 us
    all_to_all x1, starting transfers between devices, shards(): lax.all_to_all(weighted.reshape(rows, X, part).transpose(1, 0, 2), 'x', 0...  4.29 us
  transfers between devices with their start and end apart: 12, of which 9 were waited for; matrix products, arithmetic and copies ran while one was open for 0% of the time, Pallas kernels for 2%

profile of v3, /device:TPU:8, one launch (start us, length us, event | category | flops | bytes accessed | tf_op | source)
XLA Modules:
  0.0 103.6 jit_solution(15503334154397770846)
XLA Ops:
  0.7 0.7 compare_select_fusion.2
  1.3 1.0 multiply_convert_fusion
  2.4 0.7 copy.11
  3.0 4.3 %all-to-all-start = ((bf16[4,32,768]{2,1,0:T(8,128)(2,1)}), bf16[4,32,768]{2,1,0:T(8,128)(2,1)S(1)}, u32[]{:S(2)}, u32[]{:S(2)}) async-start(bf16[4,32,768]{2,1,0:T(8,128)(2,1)} %bitcast.16), calls=%async_computation | async-start | bytes 393216 | tf_op jit(solution)/shard_map/all_to_all | solution.py:126
  7.3 1.0 %copy-done = bf16[256,1024]{1,0:T(8,128)(2,1)S(1)} copy-done((bf16[256,1024]{1,0:T(8,128)(2,1)S(1)}, bf16[256,1024]{1,0:T(8,128)(2,1)}, u32[]{:S(2)}) %copy-start) | copy-done | bytes 524312
  8.4 1.0 %copy-done.1 = bf16[256,1024]{1,0:T(8,128)(2,1)S(1)} copy-done((bf16[256,1024]{1,0:T(8,128)(2,1)S(1)}, bf16[256,1024]{1,0:T(8,128)(2,1)}, u32[]{:S(2)}) %copy-start.1) | copy-done | bytes 524312
  9.4 1.0 %copy-done.2 = bf16[256,1024]{1,0:T(8,128)(2,1)S(1)} copy-done((bf16[256,1024]{1,0:T(8,128)(2,1)S(1)}, bf16[256,1024]{1,0:T(8,128)(2,1)}, u32[]{:S(2)}) %copy-start.2) | copy-done | bytes 524312
  10.5 0.8 gate_delta.1
  11.3 2.4 %all-to-all-done.rows_ref = bf16[4,32,768]{2,1,0:T(8,128)(2,1)S(1)} async-done(((bf16[4,32,768]{2,1,0:T(8,128)(2,1)}), bf16[4,32,768]{2,1,0:T(8,128)(2,1)S(1)}, u32[]{:S(2)}, u32[]{:S(2)}) %all-to-all-start) | async-done | bytes 196640 | tf_op jit(solution)/shard_map/all_to_all | solution.py:126
  13.7 3.1 %collective-permute-start.1 = (bf16[256,1024]{1,0:T(8,128)(2,1)S(1)}, bf16[256,1024]{1,0:T(8,128)(2,1)S(1)}, u32[]{:S(2)}, u32[]{:S(2)}) collective-permute-start(bf16[256,1024]{1,0:T(8,128)(2,1)S(1)} %gate_delta.1), channel_id=1, source_target_pairs={{0,384},{128,0},{256,128},{384,256},{1,385},{129,1},{257,129},{385... | collective-permute-start | bytes 1572872 | tf_op jit(solution)/shard_map/ppermute | solution.py:29
  16.7 2.8 %collective-permute-start = (bf16[256,1024]{1,0:T(8,128)(2,1)S(1)}, bf16[256,1024]{1,0:T(8,128)(2,1)S(1)}, u32[]{:S(2)}, u32[]{:S(2)}) collective-permute-start(bf16[256,1024]{1,0:T(8,128)(2,1)S(1)} %gate_delta.1), channel_id=1, source_target_pairs={{0,128},{128,256},{256,384},{384,0},{1,129},{129,257},{257,385},{3... | collective-permute-start | bytes 1572872 | tf_op jit(solution)/shard_map/ppermute | solution.py:29
  19.5 0.9 spread.1
  20.5 8.3 %all-to-all-start.1 = ((bf16[4,4,32,768]{3,2,1,0:T(8,128)(2,1)}), bf16[4,4,32,768]{3,2,1,0:T(8,128)(2,1)S(1)}, u32[]{:S(2)}, u32[]{:S(2)}) async-start(bf16[4,4,32,768]{3,2,1,0:T(8,128)(2,1)} %spread.1), calls=%async_computation.1 | async-start | bytes 1572864 | tf_op jit(solution)/shard_map/all_to_all | solution.py:148
  28.8 3.6 %collective-permute-done.before_ref = bf16[256,1024]{1,0:T(8,128)(2,1)S(1)} collective-permute-done((bf16[256,1024]{1,0:T(8,128)(2,1)S(1)}, bf16[256,1024]{1,0:T(8,128)(2,1)S(1)}, u32[]{:S(2)}, u32[]{:S(2)}) %collective-permute-start) | collective-permute-done | bytes 524320 | tf_op jit(solution)/shard_map/ppermute | solution.py:29
  32.4 1.9 %collective-permute-start.2 = (bf16[256,1024]{1,0:T(8,128)(2,1)S(1)}, bf16[256,1024]{1,0:T(8,128)(2,1)S(1)}, u32[]{:S(2)}, u32[]{:S(2)}) collective-permute-start(bf16[256,1024]{1,0:T(8,128)(2,1)S(1)} %chosen.1), channel_id=1, source_target_pairs={{0,128},{1,385},{128,256},{129,1},{256,384},{257,129},{384,0},{385... | collective-permute-start | bytes 1572872 | tf_op jit(solution)/shard_map/ppermute | solution.py:34
  34.3 2.5 %all-to-all-done.1.rows_ref = bf16[4,4,32,768]{3,2,1,0:T(8,128)(2,1)S(1)} async-done(((bf16[4,4,32,768]{3,2,1,0:T(8,128)(2,1)}), bf16[4,4,32,768]{3,2,1,0:T(8,128)(2,1)S(1)}, u32[]{:S(2)}, u32[]{:S(2)}) %all-to-all-start.1) | async-done | bytes 786464 | tf_op jit(solution)/shard_map/all_to_all | solution.py:148
  37.4 1.9 %collective-permute-start.3 = (bf16[512,768]{1,0:T(8,128)(2,1)S(1)}, bf16[512,768]{1,0:T(8,128)(2,1)S(1)}, u32[]{:S(2)}, u32[]{:S(2)}) collective-permute-start(bf16[512,768]{1,0:T(8,128)(2,1)S(1)} %ordered_rows.1), channel_id=1, source_target_pairs={{0,1},{1,0},{2,3},{3,2},{4,5},{5,4},{6,7},{7,6},{8,9},{9,8},{10,11... | collective-permute-start | bytes 2359304 | tf_op jit(solution)/shard_map/ppermute | solution.py:159
  39.5 5.2 %collective-permute-done.2 = bf16[256,1024]{1,0:T(8,128)(2,1)S(1)} collective-permute-done((bf16[256,1024]{1,0:T(8,128)(2,1)S(1)}, bf16[256,1024]{1,0:T(8,128)(2,1)S(1)}, u32[]{:S(2)}, u32[]{:S(2)}) %collective-permute-start.2) | collective-permute-done | bytes 524320 | tf_op jit(solution)/shard_map/ppermute | solution.py:34
  44.7 1.0 fusion.7
  45.8 1.0 convolution_add_fusion
  47.0 11.8 %collective-permute-start.4 = (bf16[4,48,1024]{2,1,0:T(8,128)(2,1)S(1)}, bf16[4,48,1024]{2,1,0:T(8,128)(2,1)S(1)}, u32[]{:S(2)}, u32[]{:S(2)}) collective-permute-start(bf16[4,48,1024]{2,1,0:T(8,128)(2,1)S(1)} %get-tuple-element.18), channel_id=1, source_target_pairs={{0,112},{1,17},{8,120},{9,25},{16,0},{17,33},{24,8},{25,41},{32,16... | collective-permute-start | bytes 1179656 | tf_op jit(solution)/shard_map/ppermute | solution.py:43
  58.8 2.9 %collective-permute-start.5 = (bf16[4,48,1024]{2,1,0:T(8,128)(2,1)S(1)}, bf16[4,48,1024]{2,1,0:T(8,128)(2,1)S(1)}, u32[]{:S(2)}, u32[]{:S(2)}) collective-permute-start(bf16[4,48,1024]{2,1,0:T(8,128)(2,1)S(1)} %get-tuple-element.19), channel_id=1, source_target_pairs={{0,8},{8,16},{16,24},{24,32},{32,40},{40,48},{48,56},{56,64},{64,7... | collective-permute-start | bytes 1179656 | tf_op jit(solution)/shard_map/ppermute | solution.py:38
  61.8 4.1 %collective-permute-start.6 = (bf16[4,48,1024]{2,1,0:T(8,128)(2,1)S(1)}, bf16[4,48,1024]{2,1,0:T(8,128)(2,1)S(1)}, u32[]{:S(2)}, u32[]{:S(2)}) collective-permute-start(bf16[4,48,1024]{2,1,0:T(8,128)(2,1)S(1)} %get-tuple-element.20), channel_id=1, source_target_pairs={{0,120},{8,0},{16,8},{24,16},{32,24},{40,32},{48,40},{56,48},{64,5... | collective-permute-start | bytes 1179656 | tf_op jit(solution)/shard_map/ppermute | solution.py:38
  65.9 4.7 %collective-permute-done.4.far_ref = bf16[4,48,1024]{2,1,0:T(8,128)(2,1)S(1)} collective-permute-done((bf16[4,48,1024]{2,1,0:T(8,128)(2,1)S(1)}, bf16[4,48,1024]{2,1,0:T(8,128)(2,1)S(1)}, u32[]{:S(2)}, u32[]{:S(2)}) %collective-permute-start.4) | collective-permute-done | bytes 393248 | tf_op jit(solution)/shard_map/ppermute | solution.py:43
  70.7 1.1 %collective-permute-done.5.above_ref = bf16[4,48,1024]{2,1,0:T(8,128)(2,1)S(1)} collective-permute-done((bf16[4,48,1024]{2,1,0:T(8,128)(2,1)S(1)}, bf16[4,48,1024]{2,1,0:T(8,128)(2,1)S(1)}, u32[]{:S(2)}, u32[]{:S(2)}) %collective-permute-start.5) | collective-permute-done | bytes 393248 | tf_op jit(solution)/shard_map/ppermute | solution.py:38
  71.8 3.1 %collective-permute-done.6.below_ref = bf16[4,48,1024]{2,1,0:T(8,128)(2,1)S(1)} collective-permute-done((bf16[4,48,1024]{2,1,0:T(8,128)(2,1)S(1)}, bf16[4,48,1024]{2,1,0:T(8,128)(2,1)S(1)}, u32[]{:S(2)}, u32[]{:S(2)}) %collective-permute-start.6) | collective-permute-done | bytes 393248 | tf_op jit(solution)/shard_map/ppermute | solution.py:38
  75.1 9.7 %collective-permute-start.7 = (bf16[48,1024]{1,0:T(8,128)(2,1)S(1)}, bf16[48,1024]{1,0:T(8,128)(2,1)S(1)}, u32[]{:S(2)}, u32[]{:S(2)}) collective-permute-start(bf16[48,1024]{1,0:T(8,128)(2,1)S(1)} %get-tuple-element.22), channel_id=1, source_target_pairs={{0,64},{8,72},{16,80},{24,88},{32,96},{40,104},{48,112},{56,120},{... | collective-permute-start | bytes 294920 | tf_op jit(solution)/shard_map/ppermute | solution.py:38
  84.7 5.2 %collective-permute-start.8 = (bf16[48,1024]{1,0:T(8,128)(2,1)S(1)}, bf16[48,1024]{1,0:T(8,128)(2,1)S(1)}, u32[]{:S(2)}, u32[]{:S(2)}) collective-permute-start(bf16[48,1024]{1,0:T(8,128)(2,1)S(1)} %get-tuple-element.23), channel_id=1, source_target_pairs={{0,32},{8,40},{16,48},{24,56},{32,64},{40,72},{48,80},{56,88},{64,... | collective-permute-start | bytes 294920 | tf_op jit(solution)/shard_map/ppermute | solution.py:38
  90.0 4.5 %collective-permute-start.9 = (bf16[48,1024]{1,0:T(8,128)(2,1)S(1)}, bf16[48,1024]{1,0:T(8,128)(2,1)S(1)}, u32[]{:S(2)}, u32[]{:S(2)}) collective-permute-start(bf16[48,1024]{1,0:T(8,128)(2,1)S(1)} %get-tuple-element.24), channel_id=1, source_target_pairs={{0,96},{8,104},{16,112},{24,120},{32,0},{40,8},{48,16},{56,24},{64... | collective-permute-start | bytes 294920 | tf_op jit(solution)/shard_map/ppermute | solution.py:38
  94.5 1.5 %collective-permute-done.8 = bf16[48,1024]{1,0:T(8,128)(2,1)S(1)} collective-permute-done((bf16[48,1024]{1,0:T(8,128)(2,1)S(1)}, bf16[48,1024]{1,0:T(8,128)(2,1)S(1)}, u32[]{:S(2)}, u32[]{:S(2)}) %collective-permute-start.8) | collective-permute-done | bytes 98336 | tf_op jit(solution)/shard_map/ppermute | solution.py:38
  96.0 6.9 %collective-permute-done.9 = bf16[48,1024]{1,0:T(8,128)(2,1)S(1)} collective-permute-done((bf16[48,1024]{1,0:T(8,128)(2,1)S(1)}, bf16[48,1024]{1,0:T(8,128)(2,1)S(1)}, u32[]{:S(2)}, u32[]{:S(2)}) %collective-permute-start.9) | collective-permute-done | bytes 98336 | tf_op jit(solution)/shard_map/ppermute | solution.py:38
  102.9 0.7 add_multiply_fusion
  (17 shorter events, 1.1 us)
Async XLA Ops:
  0.0 11.2 %copy-start.3 = (s32[4]{0:T(128)S(1)}, s32[4]{0:T(128)}, u32[]{:S(2)}) copy-start(s32[4]{0:T(128)} %constant.55.clone) | copy-start | bytes 52
  3.0 10.6 %all-to-all-start = ((bf16[4,32,768]{2,1,0:T(8,128)(2,1)}), bf16[4,32,768]{2,1,0:T(8,128)(2,1)S(1)}, u32[]{:S(2)}, u32[]{:S(2)}) async-start(bf16[4,32,768]{2,1,0:T(8,128)(2,1)} %bitcast.16), calls=%async_computation | async-start | bytes 393216 | tf_op jit(solution)/shard_map/all_to_all | solution.py:126
  7.3 1.0 %copy-start = (bf16[256,1024]{1,0:T(8,128)(2,1)S(1)}, bf16[256,1024]{1,0:T(8,128)(2,1)}, u32[]{:S(2)}) copy-start(bf16[256,1024]{1,0:T(8,128)(2,1)} %param.10) | copy-start | bytes 1572868
  8.4 1.0 %copy-start.1 = (bf16[256,1024]{1,0:T(8,128)(2,1)S(1)}, bf16[256,1024]{1,0:T(8,128)(2,1)}, u32[]{:S(2)}) copy-start(bf16[256,1024]{1,0:T(8,128)(2,1)} %param.11) | copy-start | bytes 1572868
  9.4 1.0 %copy-start.2 = (bf16[256,1024]{1,0:T(8,128)(2,1)S(1)}, bf16[256,1024]{1,0:T(8,128)(2,1)}, u32[]{:S(2)}) copy-start(bf16[256,1024]{1,0:T(8,128)(2,1)} %param.12) | copy-start | bytes 1572868
  13.7 15.1 %collective-permute-start.1 = (bf16[256,1024]{1,0:T(8,128)(2,1)S(1)}, bf16[256,1024]{1,0:T(8,128)(2,1)S(1)}, u32[]{:S(2)}, u32[]{:S(2)}) collective-permute-start(bf16[256,1024]{1,0:T(8,128)(2,1)S(1)} %gate_delta.1), channel_id=1, source_target_pairs={{0,384},{128,0},{256,128},{384,256},{1,385},{129,1},{257,129},{385... | collective-permute-start | bytes 1572872 | tf_op jit(solution)/shard_map/ppermute | solution.py:29
  16.7 15.6 %collective-permute-start = (bf16[256,1024]{1,0:T(8,128)(2,1)S(1)}, bf16[256,1024]{1,0:T(8,128)(2,1)S(1)}, u32[]{:S(2)}, u32[]{:S(2)}) collective-permute-start(bf16[256,1024]{1,0:T(8,128)(2,1)S(1)} %gate_delta.1), channel_id=1, source_target_pairs={{0,128},{128,256},{256,384},{384,0},{1,129},{129,257},{257,385},{3... | collective-permute-start | bytes 1572872 | tf_op jit(solution)/shard_map/ppermute | solution.py:29
  20.5 16.4 %all-to-all-start.1 = ((bf16[4,4,32,768]{3,2,1,0:T(8,128)(2,1)}), bf16[4,4,32,768]{3,2,1,0:T(8,128)(2,1)S(1)}, u32[]{:S(2)}, u32[]{:S(2)}) async-start(bf16[4,4,32,768]{3,2,1,0:T(8,128)(2,1)} %spread.1), calls=%async_computation.1 | async-start | bytes 1572864 | tf_op jit(solution)/shard_map/all_to_all | solution.py:148
  32.4 12.3 %collective-permute-start.2 = (bf16[256,1024]{1,0:T(8,128)(2,1)S(1)}, bf16[256,1024]{1,0:T(8,128)(2,1)S(1)}, u32[]{:S(2)}, u32[]{:S(2)}) collective-permute-start(bf16[256,1024]{1,0:T(8,128)(2,1)S(1)} %chosen.1), channel_id=1, source_target_pairs={{0,128},{1,385},{128,256},{129,1},{256,384},{257,129},{384,0},{385... | collective-permute-start | bytes 1572872 | tf_op jit(solution)/shard_map/ppermute | solution.py:34
  37.4 7.3 %collective-permute-start.3 = (bf16[512,768]{1,0:T(8,128)(2,1)S(1)}, bf16[512,768]{1,0:T(8,128)(2,1)S(1)}, u32[]{:S(2)}, u32[]{:S(2)}) collective-permute-start(bf16[512,768]{1,0:T(8,128)(2,1)S(1)} %ordered_rows.1), channel_id=1, source_target_pairs={{0,1},{1,0},{2,3},{3,2},{4,5},{5,4},{6,7},{7,6},{8,9},{9,8},{10,11... | collective-permute-start | bytes 2359304 | tf_op jit(solution)/shard_map/ppermute | solution.py:159
  47.0 23.7 %collective-permute-start.4 = (bf16[4,48,1024]{2,1,0:T(8,128)(2,1)S(1)}, bf16[4,48,1024]{2,1,0:T(8,128)(2,1)S(1)}, u32[]{:S(2)}, u32[]{:S(2)}) collective-permute-start(bf16[4,48,1024]{2,1,0:T(8,128)(2,1)S(1)} %get-tuple-element.18), channel_id=1, source_target_pairs={{0,112},{1,17},{8,120},{9,25},{16,0},{17,33},{24,8},{25,41},{32,16... | collective-permute-start | bytes 1179656 | tf_op jit(solution)/shard_map/ppermute | solution.py:43
  58.8 12.9 %collective-permute-start.5 = (bf16[4,48,1024]{2,1,0:T(8,128)(2,1)S(1)}, bf16[4,48,1024]{2,1,0:T(8,128)(2,1)S(1)}, u32[]{:S(2)}, u32[]{:S(2)}) collective-permute-start(bf16[4,48,1024]{2,1,0:T(8,128)(2,1)S(1)} %get-tuple-element.19), channel_id=1, source_target_pairs={{0,8},{8,16},{16,24},{24,32},{32,40},{40,48},{48,56},{56,64},{64,7... | collective-permute-start | bytes 1179656 | tf_op jit(solution)/shard_map/ppermute | solution.py:38
  61.8 13.1 %collective-permute-start.6 = (bf16[4,48,1024]{2,1,0:T(8,128)(2,1)S(1)}, bf16[4,48,1024]{2,1,0:T(8,128)(2,1)S(1)}, u32[]{:S(2)}, u32[]{:S(2)}) collective-permute-start(bf16[4,48,1024]{2,1,0:T(8,128)(2,1)S(1)} %get-tuple-element.20), channel_id=1, source_target_pairs={{0,120},{8,0},{16,8},{24,16},{32,24},{40,32},{48,40},{56,48},{64,5... | collective-permute-start | bytes 1179656 | tf_op jit(solution)/shard_map/ppermute | solution.py:38
  75.1 19.5 %collective-permute-start.7 = (bf16[48,1024]{1,0:T(8,128)(2,1)S(1)}, bf16[48,1024]{1,0:T(8,128)(2,1)S(1)}, u32[]{:S(2)}, u32[]{:S(2)}) collective-permute-start(bf16[48,1024]{1,0:T(8,128)(2,1)S(1)} %get-tuple-element.22), channel_id=1, source_target_pairs={{0,64},{8,72},{16,80},{24,88},{32,96},{40,104},{48,112},{56,120},{... | collective-permute-start | bytes 294920 | tf_op jit(solution)/shard_map/ppermute | solution.py:38
  84.7 11.3 %collective-permute-start.8 = (bf16[48,1024]{1,0:T(8,128)(2,1)S(1)}, bf16[48,1024]{1,0:T(8,128)(2,1)S(1)}, u32[]{:S(2)}, u32[]{:S(2)}) collective-permute-start(bf16[48,1024]{1,0:T(8,128)(2,1)S(1)} %get-tuple-element.23), channel_id=1, source_target_pairs={{0,32},{8,40},{16,48},{24,56},{32,64},{40,72},{48,80},{56,88},{64,... | collective-permute-start | bytes 294920 | tf_op jit(solution)/shard_map/ppermute | solution.py:38
  90.0 12.9 %collective-permute-start.9 = (bf16[48,1024]{1,0:T(8,128)(2,1)S(1)}, bf16[48,1024]{1,0:T(8,128)(2,1)S(1)}, u32[]{:S(2)}, u32[]{:S(2)}) collective-permute-start(bf16[48,1024]{1,0:T(8,128)(2,1)S(1)} %get-tuple-element.24), channel_id=1, source_target_pairs={{0,96},{8,104},{16,112},{24,120},{32,0},{40,8},{48,16},{56,24},{64... | collective-permute-start | bytes 294920 | tf_op jit(solution)/shard_map/ppermute | solution.py:38

commit v4 on v3

--- a/solution.py
+++ b/solution.py
@@ -157,12 +157,16 @@
         name="ordered_rows",
     )((x_at + jnp.array([0, X - 1, 1, 2])) % X, own)
     other = lax.ppermute(own, "c", [(0, 1), (1, 0)])
+    early = (X - 1) * half
+    terms = [
+        (rows_of[:early], [block[place * half : (place + 1) * half] for block in (delta, before, after)])
+        for place, rows_of in enumerate((own, other))
+    ]
+    terms.append((jnp.concatenate([own[early:], other[early:]], axis=0), [across]))
     product = 0.0
-    for place, tokens in enumerate((own, other)):
-        span = slice(place * half, (place + 1) * half)
-        right = [block[span] for block in (delta, before, after, across)]
+    for left, right in terms:
         product += lax.dot_general(
-            tokens,
+            left,
             jnp.concatenate(right, axis=0),
             (((0,), (0,)), ((), ())),
             preferred_element_type=jnp.float32,
@@ -179,7 +183,7 @@
         name="slabs",
     )(jnp.stack([z_at % W]), product.reshape(Z, owned, units))
 
-    far = z_apart(across_rows, 2)
+    far = z_apart(across_rows, -2)
     above = z_shift(above, 1)
     below = z_shift(below, -1)
     own_block, *blocks = pl.pallas_call(

time: 104 us -> 102 us (0.981)
  the two profiles are of different devices: /device:TPU:8 before, /device:TPU:6 now
where the time goes in v4:
time: 102 us
  starting transfers between devices  60.3 us (59%)
  waiting for transfers between devices  28.8 us (28%)
  local copies, waits for them, and re-layouts  3.95 us (4%)
  Pallas kernels  2.68 us (3%)
  matrix products  2.64 us (3%)
  other arithmetic  2.43 us (2%)
    ppermute x5, starting transfers between devices, z_shift(): return lax.ppermute(value, 'z', [(i, (i + step) % Z) for i in range(Z)])  29.7 us
    ppermute x5, waiting for transfers between devices, z_shift(): return lax.ppermute(value, 'z', [(i, (i + step) % Z) for i in range(Z)])  17.6 us
    all_to_all x1, starting transfers between devices, shards(): lax.all_to_all(weighted.reshape(rows, X, part).transpose(1, 0, 2), 'x', 0...  9.19 us
    ppermute x2, starting transfers between devices, x_shift(): return lax.ppermute(value, 'x', [(i, (i + step) % X) for i in range(X)])  7.04 us
    ppermute x1, waiting for transfers between devices, z_apart(): return lax.ppermute(value, ('z', 'c'), pairs)  5.9 us
    ppermute x1, starting transfers between devices, x_forward(): return lax.ppermute(value, ('x', 'c'), pairs)  5.59 us
    all_to_all x1, starting transfers between devices, shards(): own = lax.all_to_all(spread, 'y', 0, 0)  3.49 us
    ppermute x1, starting transfers between devices, z_apart(): return lax.ppermute(value, ('z', 'c'), pairs)  3.35 us
  transfers between devices with their start and end apart: 12, of which 9 were waited for; matrix products, arithmetic and copies ran while one was open for 2% of the time, Pallas kernels for 2%

profile of v4, /device:TPU:6, one launch (start us, length us, event | category | flops | bytes accessed | tf_op | source)
XLA Modules:
  0.0 101.7 jit_solution(13683890599881634877)
XLA Ops:
  0.7 0.7 compare_select_fusion.2
  1.3 1.0 %multiply_convert_fusion = bf16[32,3072]{1,0:T(8,128)(2,1)S(1)} fusion(bf16[32,3072]{1,0:T(8,128)(2,1)} %param.7, f32[32]{0:T(128)S(1)} %compare_select_fusion.2), kind=kLoop, calls=%fused_computation.19 | loop fusion | flops 294912 | bytes 393344 | tf_op jit(solution)/shard_map/convert_element_type | solution.py:25
  2.4 0.7 copy.11
  3.0 9.2 %all-to-all-start = ((bf16[4,32,768]{2,1,0:T(8,128)(2,1)}), bf16[4,32,768]{2,1,0:T(8,128)(2,1)S(1)}, u32[]{:S(2)}, u32[]{:S(2)}) async-start(bf16[4,32,768]{2,1,0:T(8,128)(2,1)} %bitcast.15), calls=%async_computation | async-start | bytes 393216 | tf_op jit(solution)/shard_map/all_to_all | solution.py:126
  12.2 1.0 %copy-done = bf16[256,1024]{1,0:T(8,128)(2,1)S(1)} copy-done((bf16[256,1024]{1,0:T(8,128)(2,1)S(1)}, bf16[256,1024]{1,0:T(8,128)(2,1)}, u32[]{:S(2)}) %copy-start) | copy-done | bytes 524312
  13.3 1.0 %copy-done.1 = bf16[256,1024]{1,0:T(8,128)(2,1)S(1)} copy-done((bf16[256,1024]{1,0:T(8,128)(2,1)S(1)}, bf16[256,1024]{1,0:T(8,128)(2,1)}, u32[]{:S(2)}) %copy-start.1) | copy-done | bytes 524312
  14.3 1.0 %copy-done.2 = bf16[256,1024]{1,0:T(8,128)(2,1)S(1)} copy-done((bf16[256,1024]{1,0:T(8,128)(2,1)S(1)}, bf16[256,1024]{1,0:T(8,128)(2,1)}, u32[]{:S(2)}) %copy-start.2) | copy-done | bytes 524312
  15.4 0.8 gate_delta.1
  16.5 2.4 %collective-permute-start.1 = (bf16[256,1024]{1,0:T(8,128)(2,1)S(1)}, bf16[256,1024]{1,0:T(8,128)(2,1)S(1)}, u32[]{:S(2)}, u32[]{:S(2)}) collective-permute-start(bf16[256,1024]{1,0:T(8,128)(2,1)S(1)} %gate_delta.1), channel_id=1, source_target_pairs={{0,384},{128,0},{256,128},{384,256},{1,385},{129,1},{257,129},{385... | collective-permute-start | bytes 1572872 | tf_op jit(solution)/shard_map/ppermute | solution.py:29
  18.9 4.6 %collective-permute-start = (bf16[256,1024]{1,0:T(8,128)(2,1)S(1)}, bf16[256,1024]{1,0:T(8,128)(2,1)S(1)}, u32[]{:S(2)}, u32[]{:S(2)}) collective-permute-start(bf16[256,1024]{1,0:T(8,128)(2,1)S(1)} %gate_delta.1), channel_id=1, source_target_pairs={{0,128},{128,256},{256,384},{384,0},{1,129},{129,257},{257,385},{3... | collective-permute-start | bytes 1572872 | tf_op jit(solution)/shard_map/ppermute | solution.py:29
  23.6 0.9 spread.1
  24.5 3.5 %all-to-all-start.1 = ((bf16[4,4,32,768]{3,2,1,0:T(8,128)(2,1)}), bf16[4,4,32,768]{3,2,1,0:T(8,128)(2,1)S(1)}, u32[]{:S(2)}, u32[]{:S(2)}) async-start(bf16[4,4,32,768]{3,2,1,0:T(8,128)(2,1)} %spread.1), calls=%async_computation.1 | async-start | bytes 1572864 | tf_op jit(solution)/shard_map/all_to_all | solution.py:148
  28.1 0.7 collective-permute-done.1.after_ref
  28.8 1.5 %collective-permute-done.before_ref = bf16[256,1024]{1,0:T(8,128)(2,1)S(1)} collective-permute-done((bf16[256,1024]{1,0:T(8,128)(2,1)S(1)}, bf16[256,1024]{1,0:T(8,128)(2,1)S(1)}, u32[]{:S(2)}, u32[]{:S(2)}) %collective-permute-start) | collective-permute-done | bytes 524320 | tf_op jit(solution)/shard_map/ppermute | solution.py:29
  30.3 5.6 %collective-permute-start.3 = (bf16[256,1024]{1,0:T(8,128)(2,1)S(1)}, bf16[256,1024]{1,0:T(8,128)(2,1)S(1)}, u32[]{:S(2)}, u32[]{:S(2)}) collective-permute-start(bf16[256,1024]{1,0:T(8,128)(2,1)S(1)} %chosen.1), channel_id=1, source_target_pairs={{0,128},{1,385},{128,256},{129,1},{256,384},{257,129},{384,0},{385... | collective-permute-start | bytes 1572872 | tf_op jit(solution)/shard_map/ppermute | solution.py:34
  35.9 1.6 %all-to-all-done.1.rows_ref = bf16[4,4,32,768]{3,2,1,0:T(8,128)(2,1)S(1)} async-done(((bf16[4,4,32,768]{3,2,1,0:T(8,128)(2,1)}), bf16[4,4,32,768]{3,2,1,0:T(8,128)(2,1)S(1)}, u32[]{:S(2)}, u32[]{:S(2)}) %all-to-all-start.1) | async-done | bytes 786464 | tf_op jit(solution)/shard_map/all_to_all | solution.py:148
  38.1 1.9 %collective-permute-start.2 = (bf16[512,768]{1,0:T(8,128)(2,1)S(1)}, bf16[512,768]{1,0:T(8,128)(2,1)S(1)}, u32[]{:S(2)}, u32[]{:S(2)}) collective-permute-start(bf16[512,768]{1,0:T(8,128)(2,1)S(1)} %ordered_rows.1), channel_id=1, source_target_pairs={{0,1},{1,0},{2,3},{3,2},{4,5},{5,4},{6,7},{7,6},{8,9},{9,8},{10,11... | collective-permute-start | bytes 2359304 | tf_op jit(solution)/shard_map/ppermute | solution.py:159
  40.1 1.0 fusion
  41.1 1.1 %collective-permute-done.2 = bf16[512,768]{1,0:T(8,128)(2,1)S(1)} collective-permute-done((bf16[512,768]{1,0:T(8,128)(2,1)S(1)}, bf16[512,768]{1,0:T(8,128)(2,1)S(1)}, u32[]{:S(2)}, u32[]{:S(2)}) %collective-permute-start.2) | collective-permute-done | bytes 786464 | tf_op jit(solution)/shard_map/ppermute | solution.py:159
  42.3 1.0 fusion.6
  43.3 0.6 add_add_fusion
  44.1 3.4 %collective-permute-start.4 = (bf16[4,48,1024]{2,1,0:T(8,128)(2,1)S(1)}, bf16[4,48,1024]{2,1,0:T(8,128)(2,1)S(1)}, u32[]{:S(2)}, u32[]{:S(2)}) collective-permute-start(bf16[4,48,1024]{2,1,0:T(8,128)(2,1)S(1)} %get-tuple-element.18), channel_id=1, source_target_pairs={{0,16},{1,113},{8,24},{9,121},{16,32},{17,1},{24,40},{25,9},{32,48... | collective-permute-start | bytes 1179656 | tf_op jit(solution)/shard_map/ppermute | solution.py:43
  47.5 3.8 %collective-permute-start.5 = (bf16[4,48,1024]{2,1,0:T(8,128)(2,1)S(1)}, bf16[4,48,1024]{2,1,0:T(8,128)(2,1)S(1)}, u32[]{:S(2)}, u32[]{:S(2)}) collective-permute-start(bf16[4,48,1024]{2,1,0:T(8,128)(2,1)S(1)} %get-tuple-element.19), channel_id=1, source_target_pairs={{0,8},{8,16},{16,24},{24,32},{32,40},{40,48},{48,56},{56,64},{64,7... | collective-permute-start | bytes 1179656 | tf_op jit(solution)/shard_map/ppermute | solution.py:38
  51.3 6.2 %collective-permute-start.6 = (bf16[4,48,1024]{2,1,0:T(8,128)(2,1)S(1)}, bf16[4,48,1024]{2,1,0:T(8,128)(2,1)S(1)}, u32[]{:S(2)}, u32[]{:S(2)}) collective-permute-start(bf16[4,48,1024]{2,1,0:T(8,128)(2,1)S(1)} %get-tuple-element.20), channel_id=1, source_target_pairs={{0,120},{8,0},{16,8},{24,16},{32,24},{40,32},{48,40},{56,48},{64,5... | collective-permute-start | bytes 1179656 | tf_op jit(solution)/shard_map/ppermute | solution.py:38
  57.6 5.9 %collective-permute-done.4.far_ref = bf16[4,48,1024]{2,1,0:T(8,128)(2,1)S(1)} collective-permute-done((bf16[4,48,1024]{2,1,0:T(8,128)(2,1)S(1)}, bf16[4,48,1024]{2,1,0:T(8,128)(2,1)S(1)}, u32[]{:S(2)}, u32[]{:S(2)}) %collective-permute-start.4) | collective-permute-done | bytes 393248 | tf_op jit(solution)/shard_map/ppermute | solution.py:43
  63.5 8.6 %collective-permute-done.5.above_ref = bf16[4,48,1024]{2,1,0:T(8,128)(2,1)S(1)} collective-permute-done((bf16[4,48,1024]{2,1,0:T(8,128)(2,1)S(1)}, bf16[4,48,1024]{2,1,0:T(8,128)(2,1)S(1)}, u32[]{:S(2)}, u32[]{:S(2)}) %collective-permute-start.5) | collective-permute-done | bytes 393248 | tf_op jit(solution)/shard_map/ppermute | solution.py:38
  72.2 9.9 %collective-permute-start.7 = (bf16[48,1024]{1,0:T(8,128)(2,1)S(1)}, bf16[48,1024]{1,0:T(8,128)(2,1)S(1)}, u32[]{:S(2)}, u32[]{:S(2)}) collective-permute-start(bf16[48,1024]{1,0:T(8,128)(2,1)S(1)} %get-tuple-element.22), channel_id=1, source_target_pairs={{0,64},{8,72},{16,80},{24,88},{32,96},{40,104},{48,112},{56,120},{... | collective-permute-start | bytes 294920 | tf_op jit(solution)/shard_map/ppermute | solution.py:38
  82.2 4.3 %collective-permute-start.8 = (bf16[48,1024]{1,0:T(8,128)(2,1)S(1)}, bf16[48,1024]{1,0:T(8,128)(2,1)S(1)}, u32[]{:S(2)}, u32[]{:S(2)}) collective-permute-start(bf16[48,1024]{1,0:T(8,128)(2,1)S(1)} %get-tuple-element.23), channel_id=1, source_target_pairs={{0,32},{8,40},{16,48},{24,56},{32,64},{40,72},{48,80},{56,88},{64,... | collective-permute-start | bytes 294920 | tf_op jit(solution)/shard_map/ppermute | solution.py:38
  86.5 5.5 %collective-permute-start.9 = (bf16[48,1024]{1,0:T(8,128)(2,1)S(1)}, bf16[48,1024]{1,0:T(8,128)(2,1)S(1)}, u32[]{:S(2)}, u32[]{:S(2)}) collective-permute-start(bf16[48,1024]{1,0:T(8,128)(2,1)S(1)} %get-tuple-element.24), channel_id=1, source_target_pairs={{0,96},{8,104},{16,112},{24,120},{32,0},{40,8},{48,16},{56,24},{64... | collective-permute-start | bytes 294920 | tf_op jit(solution)/shard_map/ppermute | solution.py:38
  91.9 3.2 %collective-permute-done.7 = bf16[48,1024]{1,0:T(8,128)(2,1)S(1)} collective-permute-done((bf16[48,1024]{1,0:T(8,128)(2,1)S(1)}, bf16[48,1024]{1,0:T(8,128)(2,1)S(1)}, u32[]{:S(2)}, u32[]{:S(2)}) %collective-permute-start.7) | collective-permute-done | bytes 98336 | tf_op jit(solution)/shard_map/ppermute | solution.py:38
  95.1 5.8 %collective-permute-done.9 = bf16[48,1024]{1,0:T(8,128)(2,1)S(1)} collective-permute-done((bf16[48,1024]{1,0:T(8,128)(2,1)S(1)}, bf16[48,1024]{1,0:T(8,128)(2,1)S(1)}, u32[]{:S(2)}, u32[]{:S(2)}) %collective-permute-start.9) | collective-permute-done | bytes 98336 | tf_op jit(solution)/shard_map/ppermute | solution.py:38
  100.9 0.7 add_multiply_fusion
  (19 shorter events, 1.5 us)
Async XLA Ops:
  0.0 16.1 %copy-start.3 = (s32[4]{0:T(128)S(1)}, s32[4]{0:T(128)}, u32[]{:S(2)}) copy-start(s32[4]{0:T(128)} %constant.55.clone) | copy-start | bytes 52
  3.0 13.5 %all-to-all-start = ((bf16[4,32,768]{2,1,0:T(8,128)(2,1)}), bf16[4,32,768]{2,1,0:T(8,128)(2,1)S(1)}, u32[]{:S(2)}, u32[]{:S(2)}) async-start(bf16[4,32,768]{2,1,0:T(8,128)(2,1)} %bitcast.15), calls=%async_computation | async-start | bytes 393216 | tf_op jit(solution)/shard_map/all_to_all | solution.py:126
  12.2 1.0 %copy-start = (bf16[256,1024]{1,0:T(8,128)(2,1)S(1)}, bf16[256,1024]{1,0:T(8,128)(2,1)}, u32[]{:S(2)}) copy-start(bf16[256,1024]{1,0:T(8,128)(2,1)} %param.10) | copy-start | bytes 1572868
  13.3 1.0 %copy-start.1 = (bf16[256,1024]{1,0:T(8,128)(2,1)S(1)}, bf16[256,1024]{1,0:T(8,128)(2,1)}, u32[]{:S(2)}) copy-start(bf16[256,1024]{1,0:T(8,128)(2,1)} %param.11) | copy-start | bytes 1572868
  14.3 1.0 %copy-start.2 = (bf16[256,1024]{1,0:T(8,128)(2,1)S(1)}, bf16[256,1024]{1,0:T(8,128)(2,1)}, u32[]{:S(2)}) copy-start(bf16[256,1024]{1,0:T(8,128)(2,1)} %param.12) | copy-start | bytes 1572868
  16.5 12.3 %collective-permute-start.1 = (bf16[256,1024]{1,0:T(8,128)(2,1)S(1)}, bf16[256,1024]{1,0:T(8,128)(2,1)S(1)}, u32[]{:S(2)}, u32[]{:S(2)}) collective-permute-start(bf16[256,1024]{1,0:T(8,128)(2,1)S(1)} %gate_delta.1), channel_id=1, source_target_pairs={{0,384},{128,0},{256,128},{384,256},{1,385},{129,1},{257,129},{385... | collective-permute-start | bytes 1572872 | tf_op jit(solution)/shard_map/ppermute | solution.py:29
  18.9 11.3 %collective-permute-start = (bf16[256,1024]{1,0:T(8,128)(2,1)S(1)}, bf16[256,1024]{1,0:T(8,128)(2,1)S(1)}, u32[]{:S(2)}, u32[]{:S(2)}) collective-permute-start(bf16[256,1024]{1,0:T(8,128)(2,1)S(1)} %gate_delta.1), channel_id=1, source_target_pairs={{0,128},{128,256},{256,384},{384,0},{1,129},{129,257},{257,385},{3... | collective-permute-start | bytes 1572872 | tf_op jit(solution)/shard_map/ppermute | solution.py:29
  24.5 13.0 %all-to-all-start.1 = ((bf16[4,4,32,768]{3,2,1,0:T(8,128)(2,1)}), bf16[4,4,32,768]{3,2,1,0:T(8,128)(2,1)S(1)}, u32[]{:S(2)}, u32[]{:S(2)}) async-start(bf16[4,4,32,768]{3,2,1,0:T(8,128)(2,1)} %spread.1), calls=%async_computation.1 | async-start | bytes 1572864 | tf_op jit(solution)/shard_map/all_to_all | solution.py:148
  30.3 13.0 %collective-permute-start.3 = (bf16[256,1024]{1,0:T(8,128)(2,1)S(1)}, bf16[256,1024]{1,0:T(8,128)(2,1)S(1)}, u32[]{:S(2)}, u32[]{:S(2)}) collective-permute-start(bf16[256,1024]{1,0:T(8,128)(2,1)S(1)} %chosen.1), channel_id=1, source_target_pairs={{0,128},{1,385},{128,256},{129,1},{256,384},{257,129},{384,0},{385... | collective-permute-start | bytes 1572872 | tf_op jit(solution)/shard_map/ppermute | solution.py:34
  38.1 4.2 %collective-permute-start.2 = (bf16[512,768]{1,0:T(8,128)(2,1)S(1)}, bf16[512,768]{1,0:T(8,128)(2,1)S(1)}, u32[]{:S(2)}, u32[]{:S(2)}) collective-permute-start(bf16[512,768]{1,0:T(8,128)(2,1)S(1)} %ordered_rows.1), channel_id=1, source_target_pairs={{0,1},{1,0},{2,3},{3,2},{4,5},{5,4},{6,7},{7,6},{8,9},{9,8},{10,11... | collective-permute-start | bytes 2359304 | tf_op jit(solution)/shard_map/ppermute | solution.py:159
  44.1 19.4 %collective-permute-start.4 = (bf16[4,48,1024]{2,1,0:T(8,128)(2,1)S(1)}, bf16[4,48,1024]{2,1,0:T(8,128)(2,1)S(1)}, u32[]{:S(2)}, u32[]{:S(2)}) collective-permute-start(bf16[4,48,1024]{2,1,0:T(8,128)(2,1)S(1)} %get-tuple-element.18), channel_id=1, source_target_pairs={{0,16},{1,113},{8,24},{9,121},{16,32},{17,1},{24,40},{25,9},{32,48... | collective-permute-start | bytes 1179656 | tf_op jit(solution)/shard_map/ppermute | solution.py:43
  47.5 24.6 %collective-permute-start.5 = (bf16[4,48,1024]{2,1,0:T(8,128)(2,1)S(1)}, bf16[4,48,1024]{2,1,0:T(8,128)(2,1)S(1)}, u32[]{:S(2)}, u32[]{:S(2)}) collective-permute-start(bf16[4,48,1024]{2,1,0:T(8,128)(2,1)S(1)} %get-tuple-element.19), channel_id=1, source_target_pairs={{0,8},{8,16},{16,24},{24,32},{32,40},{40,48},{48,56},{56,64},{64,7... | collective-permute-start | bytes 1179656 | tf_op jit(solution)/shard_map/ppermute | solution.py:38
  51.3 20.8 %collective-permute-start.6 = (bf16[4,48,1024]{2,1,0:T(8,128)(2,1)S(1)}, bf16[4,48,1024]{2,1,0:T(8,128)(2,1)S(1)}, u32[]{:S(2)}, u32[]{:S(2)}) collective-permute-start(bf16[4,48,1024]{2,1,0:T(8,128)(2,1)S(1)} %get-tuple-element.20), channel_id=1, source_target_pairs={{0,120},{8,0},{16,8},{24,16},{32,24},{40,32},{48,40},{56,48},{64,5... | collective-permute-start | bytes 1179656 | tf_op jit(solution)/shard_map/ppermute | solution.py:38
  72.2 22.9 %collective-permute-start.7 = (bf16[48,1024]{1,0:T(8,128)(2,1)S(1)}, bf16[48,1024]{1,0:T(8,128)(2,1)S(1)}, u32[]{:S(2)}, u32[]{:S(2)}) collective-permute-start(bf16[48,1024]{1,0:T(8,128)(2,1)S(1)} %get-tuple-element.22), channel_id=1, source_target_pairs={{0,64},{8,72},{16,80},{24,88},{32,96},{40,104},{48,112},{56,120},{... | collective-permute-start | bytes 294920 | tf_op jit(solution)/shard_map/ppermute | solution.py:38
  82.2 13.0 %collective-permute-start.8 = (bf16[48,1024]{1,0:T(8,128)(2,1)S(1)}, bf16[48,1024]{1,0:T(8,128)(2,1)S(1)}, u32[]{:S(2)}, u32[]{:S(2)}) collective-permute-start(bf16[48,1024]{1,0:T(8,128)(2,1)S(1)} %get-tuple-element.23), channel_id=1, source_target_pairs={{0,32},{8,40},{16,48},{24,56},{32,64},{40,72},{48,80},{56,88},{64,... | collective-permute-start | bytes 294920 | tf_op jit(solution)/shard_map/ppermute | solution.py:38
  86.5 14.5 %collective-permute-start.9 = (bf16[48,1024]{1,0:T(8,128)(2,1)S(1)}, bf16[48,1024]{1,0:T(8,128)(2,1)S(1)}, u32[]{:S(2)}, u32[]{:S(2)}) collective-permute-start(bf16[48,1024]{1,0:T(8,128)(2,1)S(1)} %get-tuple-element.24), channel_id=1, source_target_pairs={{0,96},{8,104},{16,112},{24,120},{32,0},{40,8},{48,16},{56,24},{64... | collective-permute-start | bytes 294920 | tf_op jit(solution)/shard_map/ppermute | solution.py:38

commit v5 on v4

--- a/solution.py
+++ b/solution.py
@@ -1,4 +1,3 @@
-import functools
 import math
 
 import jax
@@ -41,18 +40,6 @@
 def z_apart(value, step):
     pairs = [(z * C + c, (z - step + 2 * step * c) % Z * C + c) for z in range(Z) for c in range(C)]
     return lax.ppermute(value, ("z", "c"), pairs)
-
-
-def delta_kernel(at, gate_ref, up_ref, grad_ref, out_ref):
-    rows = gate_ref.shape[2]
-    for place in range(C):
-        source = (at[0] + place) % C
-        for y in range(Y):
-            gate = f32(gate_ref[y, source])
-            sigmoid_v = jax.nn.sigmoid(gate)
-            slope = sigmoid_v * (1.0 + gate * (1.0 - sigmoid_v))
-            value = f32(grad_ref[y, source]) * f32(up_ref[y, source]) * slope
-            out_ref[(place * Y + y) * rows : (place * Y + y + 1) * rows, :] = bf16(value)
 
 
 def spread_kernel(rows_ref, out_ref):
@@ -104,26 +91,23 @@
 
     live_rows = jnp.arange(rows, dtype=jnp.int32) < live_count[0]
     factor = route_weight * f32(live_rows)
-    weighted = bf16(f32(token_rows) * factor[:, None])
-    by_core = [value.reshape(Y, C, rows, units) for value in (gate_pre, up_pre, hidden_grad)]
-    tall = Y * C * rows
-    chunk = 256
-    piece = pl.BlockSpec((Y, C, rows, chunk), lambda n, at: (0, 0, 0, n))
-    delta = pl.pallas_call(
-        delta_kernel,
-        out_shape=shape((tall, units), jnp.bfloat16),
-        grid_spec=pltpu.PrefetchScalarGridSpec(
-            num_scalar_prefetch=1,
-            grid=(units // chunk,),
-            in_specs=[piece] * 3,
-            out_specs=pl.BlockSpec((tall, chunk), lambda n, at: (0, n)),
-        ),
-        compiler_params=PARAMS,
-        name="gate_delta",
-    )(jnp.stack([core]), *by_core)
+    weighted = jnp.stack(
+        [
+            bf16(f32(token_rows[:, k * part : (k + 1) * part]) * factor[:, None])
+            for k in range(X)
+        ]
+    )
+    gate = f32(gate_pre)
+    sigmoid_v = jax.nn.sigmoid(gate)
+    slope = sigmoid_v * (1.0 + gate * (1.0 - sigmoid_v))
+    delta = bf16(f32(hidden_grad) * f32(up_pre) * slope).reshape(Y, C, rows, units)
+    delta = [
+        lax.dynamic_index_in_dim(delta, place, 1, keepdims=False) for place in (core, 1 - core)
+    ]
+    delta = jnp.stack(delta).reshape(C * Y * rows, units)
 
     half = Y * rows
-    parts = lax.all_to_all(weighted.reshape(rows, X, part).transpose(1, 0, 2), "x", 0, 0)
+    parts = lax.all_to_all(weighted, "x", 0, 0)
     parts, delta = lax.optimization_barrier((parts, delta))
     before, after = x_shift(delta, 1), x_shift(delta, -1)
     chosen = pl.pallas_call(

time: 102 us -> 102 us (level)
  local copies, waits for them, and re-layouts: 3.95 us -> 0.18 us
  other arithmetic: 2.43 us -> 5.64 us
  waiting for transfers between devices: 28.8 us -> 30.3 us
    unnamed x8 -> x0, local copies, waits for them, and re-layouts: 3.13 us -> none
    another operation x0 -> x3, other arithmetic: none -> 1.73 us  [the longest x2 1.68 us: shards(): jnp.stack([bf16(f32(token_rows[:, k * part:(k + 1) * part]) * factor[:, N...]
    all_to_all x1, waiting for transfers between devices: 0.36 us -> 1.64 us  [shards(): parts = lax.all_to_all(weighted, 'x', 0, 0)]
  transfers between devices with their start and end apart: 12 -> 12, of which waited for: 9 -> 9; matrix products, arithmetic and copies ran while one was open for 2% -> 5% of each run, Pallas kernels for 2% -> 2%
where the time goes in v5:
time: 102 us; the launch traced here: 101 us
  starting transfers between devices  59.5 us (58%)
  waiting for transfers between devices  30.3 us (30%)
  other arithmetic  5.64 us (6%)
  matrix products  2.64 us (3%)
  Pallas kernels  1.91 us (2%)
    ppermute x5, starting transfers between devices, z_shift(): return lax.ppermute(value, 'z', [(i, (i + step) % Z) for i in range(Z)])  29.7 us
    ppermute x5, waiting for transfers between devices, z_shift(): return lax.ppermute(value, 'z', [(i, (i + step) % Z) for i in range(Z)])  17.6 us
    all_to_all x1, starting transfers between devices, shards(): parts = lax.all_to_all(weighted, 'x', 0, 0)  9.19 us
    ppermute x2, starting transfers between devices, x_shift(): return lax.ppermute(value, 'x', [(i, (i + step) % X) for i in range(X)])  7.04 us
    ppermute x1, waiting for transfers between devices, z_apart(): return lax.ppermute(value, ('z', 'c'), pairs)  5.92 us
    ppermute x1, starting transfers between devices, x_forward(): return lax.ppermute(value, ('x', 'c'), pairs)  5.35 us
    all_to_all x1, starting transfers between devices, shards(): own = lax.all_to_all(spread, 'y', 0, 0)  3.49 us
    ppermute x1, starting transfers between devices, z_apart(): return lax.ppermute(value, ('z', 'c'), pairs)  2.79 us
  transfers between devices with their start and end apart: 12, of which 9 were waited for; matrix products, arithmetic and copies ran while one was open for 5% of the time, Pallas kernels for 2%

profile of v5, /device:TPU:6, one launch (start us, length us, event | category | flops | bytes accessed | tf_op | source)
XLA Modules:
  0.0 101.1 jit_solution(10230387461458213276)
XLA Ops:
  0.7 0.7 compare_select_fusion.2
  1.3 1.0 fusion.27
  2.3 0.7 pad_maximum_fusion.1
  3.0 9.2 %all-to-all-start = ((bf16[4,32,768]{2,1,0:T(8,128)(2,1)}), bf16[4,32,768]{2,1,0:T(8,128)(2,1)S(1)}, u32[]{:S(2)}, u32[]{:S(2)}) async-start(bf16[4,32,768]{2,1,0:T(8,128)(2,1)} %pad_maximum_fusion.1), calls=%async_computation | async-start | bytes 393216 | tf_op jit(solution)/shard_map/all_to_all | solution.py:110
  12.2 0.7 and_select_fusion.at
  12.8 1.9 %fusion.6 = bf16[256,1024]{1,0:T(8,128)(2,1)S(1)} fusion(bf16[256,1024]{1,0:T(8,128)(2,1)} %param.10, bf16[256,1024]{1,0:T(8,128)(2,1)} %param.11, bf16[256,1024]{1,0:T(8,128)(2,1)} %param.12), kind=kLoop, calls=%fused_computation.9 | loop fusion | flops 3407872 | bytes 2097152 | tf_op jit(solution)/shard_map/convert_element_type | solution.py:24
  14.8 1.6 %all-to-all-done.rows_ref = bf16[4,32,768]{2,1,0:T(8,128)(2,1)S(1)} async-done(((bf16[4,32,768]{2,1,0:T(8,128)(2,1)}), bf16[4,32,768]{2,1,0:T(8,128)(2,1)S(1)}, u32[]{:S(2)}, u32[]{:S(2)}) %all-to-all-start) | async-done | bytes 196640 | tf_op jit(solution)/shard_map/all_to_all | solution.py:110
  16.5 2.4 %collective-permute-start.1 = (bf16[256,1024]{1,0:T(8,128)(2,1)S(1)}, bf16[256,1024]{1,0:T(8,128)(2,1)S(1)}, u32[]{:S(2)}, u32[]{:S(2)}) collective-permute-start(bf16[256,1024]{1,0:T(8,128)(2,1)S(1)} %bitcast.22), channel_id=1, source_target_pairs={{0,384},{128,0},{256,128},{384,256},{1,385},{129,1},{257,129},{385... | collective-permute-start | bytes 1572872 | tf_op jit(solution)/shard_map/ppermute | solution.py:28
  18.9 4.6 %collective-permute-start = (bf16[256,1024]{1,0:T(8,128)(2,1)S(1)}, bf16[256,1024]{1,0:T(8,128)(2,1)S(1)}, u32[]{:S(2)}, u32[]{:S(2)}) collective-permute-start(bf16[256,1024]{1,0:T(8,128)(2,1)S(1)} %bitcast.23), channel_id=1, source_target_pairs={{0,128},{128,256},{256,384},{384,0},{1,129},{129,257},{257,385},{3... | collective-permute-start | bytes 1572872 | tf_op jit(solution)/shard_map/ppermute | solution.py:28
  23.5 0.9 spread.1
  24.5 3.5 %all-to-all-start.1 = ((bf16[4,4,32,768]{3,2,1,0:T(8,128)(2,1)}), bf16[4,4,32,768]{3,2,1,0:T(8,128)(2,1)S(1)}, u32[]{:S(2)}, u32[]{:S(2)}) async-start(bf16[4,4,32,768]{3,2,1,0:T(8,128)(2,1)} %spread.1), calls=%async_computation.1 | async-start | bytes 1572864 | tf_op jit(solution)/shard_map/all_to_all | solution.py:132
  28.0 0.7 collective-permute-done.1.after_ref
  28.7 1.7 %collective-permute-done.before_ref = bf16[256,1024]{1,0:T(8,128)(2,1)S(1)} collective-permute-done((bf16[256,1024]{1,0:T(8,128)(2,1)S(1)}, bf16[256,1024]{1,0:T(8,128)(2,1)S(1)}, u32[]{:S(2)}, u32[]{:S(2)}) %collective-permute-start) | collective-permute-done | bytes 524320 | tf_op jit(solution)/shard_map/ppermute | solution.py:28
  30.5 5.4 %collective-permute-start.3 = (bf16[256,1024]{1,0:T(8,128)(2,1)S(1)}, bf16[256,1024]{1,0:T(8,128)(2,1)S(1)}, u32[]{:S(2)}, u32[]{:S(2)}) collective-permute-start(bf16[256,1024]{1,0:T(8,128)(2,1)S(1)} %chosen.1), channel_id=1, source_target_pairs={{0,128},{1,385},{128,256},{129,1},{256,384},{257,129},{384,0},{385... | collective-permute-start | bytes 1572872 | tf_op jit(solution)/shard_map/ppermute | solution.py:33
  35.9 1.6 %all-to-all-done.1.rows_ref = bf16[4,4,32,768]{3,2,1,0:T(8,128)(2,1)S(1)} async-done(((bf16[4,4,32,768]{3,2,1,0:T(8,128)(2,1)}), bf16[4,4,32,768]{3,2,1,0:T(8,128)(2,1)S(1)}, u32[]{:S(2)}, u32[]{:S(2)}) %all-to-all-start.1) | async-done | bytes 786464 | tf_op jit(solution)/shard_map/all_to_all | solution.py:132
  37.4 0.6 ordered_rows.1
  38.0 1.9 %collective-permute-start.2 = (bf16[512,768]{1,0:T(8,128)(2,1)S(1)}, bf16[512,768]{1,0:T(8,128)(2,1)S(1)}, u32[]{:S(2)}, u32[]{:S(2)}) collective-permute-start(bf16[512,768]{1,0:T(8,128)(2,1)S(1)} %ordered_rows.1), channel_id=1, source_target_pairs={{0,1},{1,0},{2,3},{3,2},{4,5},{5,4},{6,7},{7,6},{8,9},{9,8},{10,11... | collective-permute-start | bytes 2359304 | tf_op jit(solution)/shard_map/ppermute | solution.py:143
  40.1 1.0 %fusion.7 = f32[768,1024]{1,0:T(8,128)S(1)} fusion(bf16[128,1024]{1,0:T(8,128)(2,1)S(1)} %get-tuple-element.30, bf16[128,1024]{1,0:T(8,128)(2,1)S(1)} %get-tuple-element.28, bf16[128,1024]{1,0:T(8,128)(2,1)S(1)} %get-tuple-element.26, bf16[512,768]{1,0:T(8,128)(2,1)S(1)} %ordered_rows.1), kind=kOutput, calls=%fused_computation.10 | convolution fusion | flops 606339072 | bytes 4521984 | tf_op jit(solution)/shard_map/dot_general | solution.py:152
  41.1 1.1 %collective-permute-done.2 = bf16[512,768]{1,0:T(8,128)(2,1)S(1)} collective-permute-done((bf16[512,768]{1,0:T(8,128)(2,1)S(1)}, bf16[512,768]{1,0:T(8,128)(2,1)S(1)}, u32[]{:S(2)}, u32[]{:S(2)}) %collective-permute-start.2) | collective-permute-done | bytes 786464 | tf_op jit(solution)/shard_map/ppermute | solution.py:143
  42.2 1.0 %fusion.13 = f32[768,1024]{1,0:T(8,128)S(1)} fusion(bf16[128,1024]{1,0:T(8,128)(2,1)S(1)} %get-tuple-element.29, bf16[128,1024]{1,0:T(8,128)(2,1)S(1)} %get-tuple-element.27, bf16[128,1024]{1,0:T(8,128)(2,1)S(1)} %get-tuple-element.25, bf16[512,768]{1,0:T(8,128)(2,1)S(1)} %collective-permute-done.2), kind=kOutput, calls=%fused_computation.16 | convolution fusion | flops 606339072 | bytes 4521984 | tf_op jit(solution)/shard_map/dot_general | solution.py:152
  43.2 0.6 add_add_fusion
  44.0 2.8 %collective-permute-start.4 = (bf16[4,48,1024]{2,1,0:T(8,128)(2,1)S(1)}, bf16[4,48,1024]{2,1,0:T(8,128)(2,1)S(1)}, u32[]{:S(2)}, u32[]{:S(2)}) collective-permute-start(bf16[4,48,1024]{2,1,0:T(8,128)(2,1)S(1)} %get-tuple-element.18), channel_id=1, source_target_pairs={{0,16},{1,113},{8,24},{9,121},{16,32},{17,1},{24,40},{25,9},{32,48... | collective-permute-start | bytes 1179656 | tf_op jit(solution)/shard_map/ppermute | solution.py:42
  46.8 3.8 %collective-permute-start.5 = (bf16[4,48,1024]{2,1,0:T(8,128)(2,1)S(1)}, bf16[4,48,1024]{2,1,0:T(8,128)(2,1)S(1)}, u32[]{:S(2)}, u32[]{:S(2)}) collective-permute-start(bf16[4,48,1024]{2,1,0:T(8,128)(2,1)S(1)} %get-tuple-element.19), channel_id=1, source_target_pairs={{0,8},{8,16},{16,24},{24,32},{32,40},{40,48},{48,56},{56,64},{64,7... | collective-permute-start | bytes 1179656 | tf_op jit(solution)/shard_map/ppermute | solution.py:37
  50.7 6.2 %collective-permute-start.6 = (bf16[4,48,1024]{2,1,0:T(8,128)(2,1)S(1)}, bf16[4,48,1024]{2,1,0:T(8,128)(2,1)S(1)}, u32[]{:S(2)}, u32[]{:S(2)}) collective-permute-start(bf16[4,48,1024]{2,1,0:T(8,128)(2,1)S(1)} %get-tuple-element.20), channel_id=1, source_target_pairs={{0,120},{8,0},{16,8},{24,16},{32,24},{40,32},{48,40},{56,48},{64,5... | collective-permute-start | bytes 1179656 | tf_op jit(solution)/shard_map/ppermute | solution.py:37
  56.9 5.9 %collective-permute-done.4.far_ref = bf16[4,48,1024]{2,1,0:T(8,128)(2,1)S(1)} collective-permute-done((bf16[4,48,1024]{2,1,0:T(8,128)(2,1)S(1)}, bf16[4,48,1024]{2,1,0:T(8,128)(2,1)S(1)}, u32[]{:S(2)}, u32[]{:S(2)}) %collective-permute-start.4) | collective-permute-done | bytes 393248 | tf_op jit(solution)/shard_map/ppermute | solution.py:42
  62.9 8.6 %collective-permute-done.5.above_ref = bf16[4,48,1024]{2,1,0:T(8,128)(2,1)S(1)} collective-permute-done((bf16[4,48,1024]{2,1,0:T(8,128)(2,1)S(1)}, bf16[4,48,1024]{2,1,0:T(8,128)(2,1)S(1)}, u32[]{:S(2)}, u32[]{:S(2)}) %collective-permute-start.5) | collective-permute-done | bytes 393248 | tf_op jit(solution)/shard_map/ppermute | solution.py:37
  71.6 9.9 %collective-permute-start.7 = (bf16[48,1024]{1,0:T(8,128)(2,1)S(1)}, bf16[48,1024]{1,0:T(8,128)(2,1)S(1)}, u32[]{:S(2)}, u32[]{:S(2)}) collective-permute-start(bf16[48,1024]{1,0:T(8,128)(2,1)S(1)} %get-tuple-element.22), channel_id=1, source_target_pairs={{0,64},{8,72},{16,80},{24,88},{32,96},{40,104},{48,112},{56,120},{... | collective-permute-start | bytes 294920 | tf_op jit(solution)/shard_map/ppermute | solution.py:37
  81.5 4.3 %collective-permute-start.8 = (bf16[48,1024]{1,0:T(8,128)(2,1)S(1)}, bf16[48,1024]{1,0:T(8,128)(2,1)S(1)}, u32[]{:S(2)}, u32[]{:S(2)}) collective-permute-start(bf16[48,1024]{1,0:T(8,128)(2,1)S(1)} %get-tuple-element.23), channel_id=1, source_target_pairs={{0,32},{8,40},{16,48},{24,56},{32,64},{40,72},{48,80},{56,88},{64,... | collective-permute-start | bytes 294920 | tf_op jit(solution)/shard_map/ppermute | solution.py:37
  85.8 5.5 %collective-permute-start.9 = (bf16[48,1024]{1,0:T(8,128)(2,1)S(1)}, bf16[48,1024]{1,0:T(8,128)(2,1)S(1)}, u32[]{:S(2)}, u32[]{:S(2)}) collective-permute-start(bf16[48,1024]{1,0:T(8,128)(2,1)S(1)} %get-tuple-element.24), channel_id=1, source_target_pairs={{0,96},{8,104},{16,112},{24,120},{32,0},{40,8},{48,16},{56,24},{64... | collective-permute-start | bytes 294920 | tf_op jit(solution)/shard_map/ppermute | solution.py:37
  91.3 3.2 %collective-permute-done.7 = bf16[48,1024]{1,0:T(8,128)(2,1)S(1)} collective-permute-done((bf16[48,1024]{1,0:T(8,128)(2,1)S(1)}, bf16[48,1024]{1,0:T(8,128)(2,1)S(1)}, u32[]{:S(2)}, u32[]{:S(2)}) %collective-permute-start.7) | collective-permute-done | bytes 98336 | tf_op jit(solution)/shard_map/ppermute | solution.py:37
  94.5 5.8 %collective-permute-done.9 = bf16[48,1024]{1,0:T(8,128)(2,1)S(1)} collective-permute-done((bf16[48,1024]{1,0:T(8,128)(2,1)S(1)}, bf16[48,1024]{1,0:T(8,128)(2,1)S(1)}, u32[]{:S(2)}, u32[]{:S(2)}) %collective-permute-start.9) | collective-permute-done | bytes 98336 | tf_op jit(solution)/shard_map/ppermute | solution.py:37
  100.3 0.7 add_multiply_fusion
  (13 shorter events, 0.6 us)
Async XLA Ops:
  3.0 13.5 %all-to-all-start = ((bf16[4,32,768]{2,1,0:T(8,128)(2,1)}), bf16[4,32,768]{2,1,0:T(8,128)(2,1)S(1)}, u32[]{:S(2)}, u32[]{:S(2)}) async-start(bf16[4,32,768]{2,1,0:T(8,128)(2,1)} %pad_maximum_fusion.1), calls=%async_computation | async-start | bytes 393216 | tf_op jit(solution)/shard_map/all_to_all | solution.py:110
  16.5 12.3 %collective-permute-start.1 = (bf16[256,1024]{1,0:T(8,128)(2,1)S(1)}, bf16[256,1024]{1,0:T(8,128)(2,1)S(1)}, u32[]{:S(2)}, u32[]{:S(2)}) collective-permute-start(bf16[256,1024]{1,0:T(8,128)(2,1)S(1)} %bitcast.22), channel_id=1, source_target_pairs={{0,384},{128,0},{256,128},{384,256},{1,385},{129,1},{257,129},{385... | collective-permute-start | bytes 1572872 | tf_op jit(solution)/shard_map/ppermute | solution.py:28
  18.9 11.6 %collective-permute-start = (bf16[256,1024]{1,0:T(8,128)(2,1)S(1)}, bf16[256,1024]{1,0:T(8,128)(2,1)S(1)}, u32[]{:S(2)}, u32[]{:S(2)}) collective-permute-start(bf16[256,1024]{1,0:T(8,128)(2,1)S(1)} %bitcast.23), channel_id=1, source_target_pairs={{0,128},{128,256},{256,384},{384,0},{1,129},{129,257},{257,385},{3... | collective-permute-start | bytes 1572872 | tf_op jit(solution)/shard_map/ppermute | solution.py:28
  24.5 13.0 %all-to-all-start.1 = ((bf16[4,4,32,768]{3,2,1,0:T(8,128)(2,1)}), bf16[4,4,32,768]{3,2,1,0:T(8,128)(2,1)S(1)}, u32[]{:S(2)}, u32[]{:S(2)}) async-start(bf16[4,4,32,768]{3,2,1,0:T(8,128)(2,1)} %spread.1), calls=%async_computation.1 | async-start | bytes 1572864 | tf_op jit(solution)/shard_map/all_to_all | solution.py:132
  30.5 12.7 %collective-permute-start.3 = (bf16[256,1024]{1,0:T(8,128)(2,1)S(1)}, bf16[256,1024]{1,0:T(8,128)(2,1)S(1)}, u32[]{:S(2)}, u32[]{:S(2)}) collective-permute-start(bf16[256,1024]{1,0:T(8,128)(2,1)S(1)} %chosen.1), channel_id=1, source_target_pairs={{0,128},{1,385},{128,256},{129,1},{256,384},{257,129},{384,0},{385... | collective-permute-start | bytes 1572872 | tf_op jit(solution)/shard_map/ppermute | solution.py:33
  38.0 4.2 %collective-permute-start.2 = (bf16[512,768]{1,0:T(8,128)(2,1)S(1)}, bf16[512,768]{1,0:T(8,128)(2,1)S(1)}, u32[]{:S(2)}, u32[]{:S(2)}) collective-permute-start(bf16[512,768]{1,0:T(8,128)(2,1)S(1)} %ordered_rows.1), channel_id=1, source_target_pairs={{0,1},{1,0},{2,3},{3,2},{4,5},{5,4},{6,7},{7,6},{8,9},{9,8},{10,11... | collective-permute-start | bytes 2359304 | tf_op jit(solution)/shard_map/ppermute | solution.py:143
  44.0 18.8 %collective-permute-start.4 = (bf16[4,48,1024]{2,1,0:T(8,128)(2,1)S(1)}, bf16[4,48,1024]{2,1,0:T(8,128)(2,1)S(1)}, u32[]{:S(2)}, u32[]{:S(2)}) collective-permute-start(bf16[4,48,1024]{2,1,0:T(8,128)(2,1)S(1)} %get-tuple-element.18), channel_id=1, source_target_pairs={{0,16},{1,113},{8,24},{9,121},{16,32},{17,1},{24,40},{25,9},{32,48... | collective-permute-start | bytes 1179656 | tf_op jit(solution)/shard_map/ppermute | solution.py:42
  46.8 24.6 %collective-permute-start.5 = (bf16[4,48,1024]{2,1,0:T(8,128)(2,1)S(1)}, bf16[4,48,1024]{2,1,0:T(8,128)(2,1)S(1)}, u32[]{:S(2)}, u32[]{:S(2)}) collective-permute-start(bf16[4,48,1024]{2,1,0:T(8,128)(2,1)S(1)} %get-tuple-element.19), channel_id=1, source_target_pairs={{0,8},{8,16},{16,24},{24,32},{32,40},{40,48},{48,56},{56,64},{64,7... | collective-permute-start | bytes 1179656 | tf_op jit(solution)/shard_map/ppermute | solution.py:37
  50.7 20.8 %collective-permute-start.6 = (bf16[4,48,1024]{2,1,0:T(8,128)(2,1)S(1)}, bf16[4,48,1024]{2,1,0:T(8,128)(2,1)S(1)}, u32[]{:S(2)}, u32[]{:S(2)}) collective-permute-start(bf16[4,48,1024]{2,1,0:T(8,128)(2,1)S(1)} %get-tuple-element.20), channel_id=1, source_target_pairs={{0,120},{8,0},{16,8},{24,16},{32,24},{40,32},{48,40},{56,48},{64,5... | collective-permute-start | bytes 1179656 | tf_op jit(solution)/shard_map/ppermute | solution.py:37
  71.6 22.9 %collective-permute-start.7 = (bf16[48,1024]{1,0:T(8,128)(2,1)S(1)}, bf16[48,1024]{1,0:T(8,128)(2,1)S(1)}, u32[]{:S(2)}, u32[]{:S(2)}) collective-permute-start(bf16[48,1024]{1,0:T(8,128)(2,1)S(1)} %get-tuple-element.22), channel_id=1, source_target_pairs={{0,64},{8,72},{16,80},{24,88},{32,96},{40,104},{48,112},{56,120},{... | collective-permute-start | bytes 294920 | tf_op jit(solution)/shard_map/ppermute | solution.py:37
  81.5 13.0 %collective-permute-start.8 = (bf16[48,1024]{1,0:T(8,128)(2,1)S(1)}, bf16[48,1024]{1,0:T(8,128)(2,1)S(1)}, u32[]{:S(2)}, u32[]{:S(2)}) collective-permute-start(bf16[48,1024]{1,0:T(8,128)(2,1)S(1)} %get-tuple-element.23), channel_id=1, source_target_pairs={{0,32},{8,40},{16,48},{24,56},{32,64},{40,72},{48,80},{56,88},{64,... | collective-permute-start | bytes 294920 | tf_op jit(solution)/shard_map/ppermute | solution.py:37
  85.8 14.5 %collective-permute-start.9 = (bf16[48,1024]{1,0:T(8,128)(2,1)S(1)}, bf16[48,1024]{1,0:T(8,128)(2,1)S(1)}, u32[]{:S(2)}, u32[]{:S(2)}) collective-permute-start(bf16[48,1024]{1,0:T(8,128)(2,1)S(1)} %get-tuple-element.24), channel_id=1, source_target_pairs={{0,96},{8,104},{16,112},{24,120},{32,0},{40,8},{48,16},{56,24},{64... | collective-permute-start | bytes 294920 | tf_op jit(solution)/shard_map/ppermute | solution.py:37

commit v6 on v5

--- a/solution.py
+++ b/solution.py
@@ -89,13 +89,10 @@
     z_at = lax.axis_index("z")
     shape = jax.ShapeDtypeStruct
 
-    live_rows = jnp.arange(rows, dtype=jnp.int32) < live_count[0]
-    factor = route_weight * f32(live_rows)
+    live = lax.broadcasted_iota(jnp.int32, (rows, part), 0) < live_count[0]
+    factor = jnp.broadcast_to(route_weight[:, None], (rows, part)) * f32(live)
     weighted = jnp.stack(
-        [
-            bf16(f32(token_rows[:, k * part : (k + 1) * part]) * factor[:, None])
-            for k in range(X)
-        ]
+        [bf16(f32(token_rows[:, k * part : (k + 1) * part]) * factor) for k in range(X)]
     )
     gate = f32(gate_pre)
     sigmoid_v = jax.nn.sigmoid(gate)

time: 102 us -> 101 us (level)
  no operation moved by 1% of the time
where the time goes in v6:
time: 101 us; the launch traced here: 100 us
  starting transfers between devices  59.5 us (59%)
  waiting for transfers between devices  30.3 us (30%)
  other arithmetic  5.01 us (5%)
  matrix products  2.64 us (3%)
  Pallas kernels  1.91 us (2%)
    ppermute x5, starting transfers between devices, z_shift(): return lax.ppermute(value, 'z', [(i, (i + step) % Z) for i in range(Z)])  29.7 us
    ppermute x5, waiting for transfers between devices, z_shift(): return lax.ppermute(value, 'z', [(i, (i + step) % Z) for i in range(Z)])  17.6 us
    all_to_all x1, starting transfers between devices, shards(): parts = lax.all_to_all(weighted, 'x', 0, 0)  9.19 us
    ppermute x2, starting transfers between devices, x_shift(): return lax.ppermute(value, 'x', [(i, (i + step) % X) for i in range(X)])  7.04 us
    ppermute x1, waiting for transfers between devices, z_apart(): return lax.ppermute(value, ('z', 'c'), pairs)  5.92 us
    ppermute x1, starting transfers between devices, x_forward(): return lax.ppermute(value, ('x', 'c'), pairs)  5.35 us
    all_to_all x1, starting transfers between devices, shards(): own = lax.all_to_all(spread, 'y', 0, 0)  3.49 us
    ppermute x1, starting transfers between devices, z_apart(): return lax.ppermute(value, ('z', 'c'), pairs)  2.8 us
  transfers between devices with their start and end apart: 12, of which 9 were waited for; matrix products, arithmetic and copies ran while one was open for 5% of the time, Pallas kernels for 2%

profile of v6, /device:TPU:6, one launch (start us, length us, event | category | flops | bytes accessed | tf_op | source)
XLA Modules:
  0.0 100.4 jit_solution(1951831209196460285)
XLA Ops:
  0.7 1.0 fusion.34
  1.7 0.7 pad_maximum_fusion.1
  2.4 9.2 %all-to-all-start = ((bf16[4,32,768]{2,1,0:T(8,128)(2,1)}), bf16[4,32,768]{2,1,0:T(8,128)(2,1)S(1)}, u32[]{:S(2)}, u32[]{:S(2)}) async-start(bf16[4,32,768]{2,1,0:T(8,128)(2,1)} %pad_maximum_fusion.1), calls=%async_computation | async-start | bytes 393216 | tf_op jit(solution)/shard_map/all_to_all | solution.py:107
  11.6 0.7 and_select_fusion.at
  12.2 1.9 %fusion.6 = bf16[256,1024]{1,0:T(8,128)(2,1)S(1)} fusion(bf16[256,1024]{1,0:T(8,128)(2,1)} %param.10, bf16[256,1024]{1,0:T(8,128)(2,1)} %param.11, bf16[256,1024]{1,0:T(8,128)(2,1)} %param.12), kind=kLoop, calls=%fused_computation.9 | loop fusion | flops 3407872 | bytes 2097152 | tf_op jit(solution)/shard_map/convert_element_type | solution.py:24
  14.2 1.6 %all-to-all-done.rows_ref = bf16[4,32,768]{2,1,0:T(8,128)(2,1)S(1)} async-done(((bf16[4,32,768]{2,1,0:T(8,128)(2,1)}), bf16[4,32,768]{2,1,0:T(8,128)(2,1)S(1)}, u32[]{:S(2)}, u32[]{:S(2)}) %all-to-all-start) | async-done | bytes 196640 | tf_op jit(solution)/shard_map/all_to_all | solution.py:107
  15.8 2.4 %collective-permute-start.1 = (bf16[256,1024]{1,0:T(8,128)(2,1)S(1)}, bf16[256,1024]{1,0:T(8,128)(2,1)S(1)}, u32[]{:S(2)}, u32[]{:S(2)}) collective-permute-start(bf16[256,1024]{1,0:T(8,128)(2,1)S(1)} %bitcast.22), channel_id=1, source_target_pairs={{0,384},{128,0},{256,128},{384,256},{1,385},{129,1},{257,129},{385... | collective-permute-start | bytes 1572872 | tf_op jit(solution)/shard_map/ppermute | solution.py:28
  18.3 4.6 %collective-permute-start = (bf16[256,1024]{1,0:T(8,128)(2,1)S(1)}, bf16[256,1024]{1,0:T(8,128)(2,1)S(1)}, u32[]{:S(2)}, u32[]{:S(2)}) collective-permute-start(bf16[256,1024]{1,0:T(8,128)(2,1)S(1)} %bitcast.23), channel_id=1, source_target_pairs={{0,128},{128,256},{256,384},{384,0},{1,129},{129,257},{257,385},{3... | collective-permute-start | bytes 1572872 | tf_op jit(solution)/shard_map/ppermute | solution.py:28
  22.9 0.9 spread.1
  23.8 3.5 %all-to-all-start.1 = ((bf16[4,4,32,768]{3,2,1,0:T(8,128)(2,1)}), bf16[4,4,32,768]{3,2,1,0:T(8,128)(2,1)S(1)}, u32[]{:S(2)}, u32[]{:S(2)}) async-start(bf16[4,4,32,768]{3,2,1,0:T(8,128)(2,1)} %spread.1), calls=%async_computation.1 | async-start | bytes 1572864 | tf_op jit(solution)/shard_map/all_to_all | solution.py:129
  27.4 0.7 collective-permute-done.1.after_ref
  28.1 1.7 %collective-permute-done.before_ref = bf16[256,1024]{1,0:T(8,128)(2,1)S(1)} collective-permute-done((bf16[256,1024]{1,0:T(8,128)(2,1)S(1)}, bf16[256,1024]{1,0:T(8,128)(2,1)S(1)}, u32[]{:S(2)}, u32[]{:S(2)}) %collective-permute-start) | collective-permute-done | bytes 524320 | tf_op jit(solution)/shard_map/ppermute | solution.py:28
  29.9 5.4 %collective-permute-start.3 = (bf16[256,1024]{1,0:T(8,128)(2,1)S(1)}, bf16[256,1024]{1,0:T(8,128)(2,1)S(1)}, u32[]{:S(2)}, u32[]{:S(2)}) collective-permute-start(bf16[256,1024]{1,0:T(8,128)(2,1)S(1)} %chosen.1), channel_id=1, source_target_pairs={{0,128},{1,385},{128,256},{129,1},{256,384},{257,129},{384,0},{385... | collective-permute-start | bytes 1572872 | tf_op jit(solution)/shard_map/ppermute | solution.py:33
  35.2 1.6 %all-to-all-done.1.rows_ref = bf16[4,4,32,768]{3,2,1,0:T(8,128)(2,1)S(1)} async-done(((bf16[4,4,32,768]{3,2,1,0:T(8,128)(2,1)}), bf16[4,4,32,768]{3,2,1,0:T(8,128)(2,1)S(1)}, u32[]{:S(2)}, u32[]{:S(2)}) %all-to-all-start.1) | async-done | bytes 786464 | tf_op jit(solution)/shard_map/all_to_all | solution.py:129
  36.8 0.6 ordered_rows.1
  37.4 1.9 %collective-permute-start.2 = (bf16[512,768]{1,0:T(8,128)(2,1)S(1)}, bf16[512,768]{1,0:T(8,128)(2,1)S(1)}, u32[]{:S(2)}, u32[]{:S(2)}) collective-permute-start(bf16[512,768]{1,0:T(8,128)(2,1)S(1)} %ordered_rows.1), channel_id=1, source_target_pairs={{0,1},{1,0},{2,3},{3,2},{4,5},{5,4},{6,7},{7,6},{8,9},{9,8},{10,11... | collective-permute-start | bytes 2359304 | tf_op jit(solution)/shard_map/ppermute | solution.py:140
  39.4 1.0 %fusion.7 = f32[768,1024]{1,0:T(8,128)S(1)} fusion(bf16[128,1024]{1,0:T(8,128)(2,1)S(1)} %get-tuple-element.30, bf16[128,1024]{1,0:T(8,128)(2,1)S(1)} %get-tuple-element.28, bf16[128,1024]{1,0:T(8,128)(2,1)S(1)} %get-tuple-element.26, bf16[512,768]{1,0:T(8,128)(2,1)S(1)} %ordered_rows.1), kind=kOutput, calls=%fused_computation.10 | convolution fusion | flops 606339072 | bytes 4521984 | tf_op jit(solution)/shard_map/dot_general | solution.py:149
  40.5 1.1 %collective-permute-done.2 = bf16[512,768]{1,0:T(8,128)(2,1)S(1)} collective-permute-done((bf16[512,768]{1,0:T(8,128)(2,1)S(1)}, bf16[512,768]{1,0:T(8,128)(2,1)S(1)}, u32[]{:S(2)}, u32[]{:S(2)}) %collective-permute-start.2) | collective-permute-done | bytes 786464 | tf_op jit(solution)/shard_map/ppermute | solution.py:140
  41.6 1.0 %fusion.13 = f32[768,1024]{1,0:T(8,128)S(1)} fusion(bf16[128,1024]{1,0:T(8,128)(2,1)S(1)} %get-tuple-element.29, bf16[128,1024]{1,0:T(8,128)(2,1)S(1)} %get-tuple-element.27, bf16[128,1024]{1,0:T(8,128)(2,1)S(1)} %get-tuple-element.25, bf16[512,768]{1,0:T(8,128)(2,1)S(1)} %collective-permute-done.2), kind=kOutput, calls=%fused_computation.16 | convolution fusion | flops 606339072 | bytes 4521984 | tf_op jit(solution)/shard_map/dot_general | solution.py:149
  42.6 0.6 add_add_fusion
  43.2 0.2 slabs.1
  43.4 2.8 %collective-permute-start.4 = (bf16[4,48,1024]{2,1,0:T(8,128)(2,1)S(1)}, bf16[4,48,1024]{2,1,0:T(8,128)(2,1)S(1)}, u32[]{:S(2)}, u32[]{:S(2)}) collective-permute-start(bf16[4,48,1024]{2,1,0:T(8,128)(2,1)S(1)} %get-tuple-element.18), channel_id=1, source_target_pairs={{0,16},{1,113},{8,24},{9,121},{16,32},{17,1},{24,40},{25,9},{32,48... | collective-permute-start | bytes 1179656 | tf_op jit(solution)/shard_map/ppermute | solution.py:42
  46.2 3.8 %collective-permute-start.5 = (bf16[4,48,1024]{2,1,0:T(8,128)(2,1)S(1)}, bf16[4,48,1024]{2,1,0:T(8,128)(2,1)S(1)}, u32[]{:S(2)}, u32[]{:S(2)}) collective-permute-start(bf16[4,48,1024]{2,1,0:T(8,128)(2,1)S(1)} %get-tuple-element.19), channel_id=1, source_target_pairs={{0,8},{8,16},{16,24},{24,32},{32,40},{40,48},{48,56},{56,64},{64,7... | collective-permute-start | bytes 1179656 | tf_op jit(solution)/shard_map/ppermute | solution.py:37
  50.1 6.2 %collective-permute-start.6 = (bf16[4,48,1024]{2,1,0:T(8,128)(2,1)S(1)}, bf16[4,48,1024]{2,1,0:T(8,128)(2,1)S(1)}, u32[]{:S(2)}, u32[]{:S(2)}) collective-permute-start(bf16[4,48,1024]{2,1,0:T(8,128)(2,1)S(1)} %get-tuple-element.20), channel_id=1, source_target_pairs={{0,120},{8,0},{16,8},{24,16},{32,24},{40,32},{48,40},{56,48},{64,5... | collective-permute-start | bytes 1179656 | tf_op jit(solution)/shard_map/ppermute | solution.py:37
  56.3 5.9 %collective-permute-done.4.far_ref = bf16[4,48,1024]{2,1,0:T(8,128)(2,1)S(1)} collective-permute-done((bf16[4,48,1024]{2,1,0:T(8,128)(2,1)S(1)}, bf16[4,48,1024]{2,1,0:T(8,128)(2,1)S(1)}, u32[]{:S(2)}, u32[]{:S(2)}) %collective-permute-start.4) | collective-permute-done | bytes 393248 | tf_op jit(solution)/shard_map/ppermute | solution.py:42
  62.2 8.6 %collective-permute-done.5.above_ref = bf16[4,48,1024]{2,1,0:T(8,128)(2,1)S(1)} collective-permute-done((bf16[4,48,1024]{2,1,0:T(8,128)(2,1)S(1)}, bf16[4,48,1024]{2,1,0:T(8,128)(2,1)S(1)}, u32[]{:S(2)}, u32[]{:S(2)}) %collective-permute-start.5) | collective-permute-done | bytes 393248 | tf_op jit(solution)/shard_map/ppermute | solution.py:37
  71.0 9.9 %collective-permute-start.7 = (bf16[48,1024]{1,0:T(8,128)(2,1)S(1)}, bf16[48,1024]{1,0:T(8,128)(2,1)S(1)}, u32[]{:S(2)}, u32[]{:S(2)}) collective-permute-start(bf16[48,1024]{1,0:T(8,128)(2,1)S(1)} %get-tuple-element.22), channel_id=1, source_target_pairs={{0,64},{8,72},{16,80},{24,88},{32,96},{40,104},{48,112},{56,120},{... | collective-permute-start | bytes 294920 | tf_op jit(solution)/shard_map/ppermute | solution.py:37
  80.9 4.3 %collective-permute-start.8 = (bf16[48,1024]{1,0:T(8,128)(2,1)S(1)}, bf16[48,1024]{1,0:T(8,128)(2,1)S(1)}, u32[]{:S(2)}, u32[]{:S(2)}) collective-permute-start(bf16[48,1024]{1,0:T(8,128)(2,1)S(1)} %get-tuple-element.23), channel_id=1, source_target_pairs={{0,32},{8,40},{16,48},{24,56},{32,64},{40,72},{48,80},{56,88},{64,... | collective-permute-start | bytes 294920 | tf_op jit(solution)/shard_map/ppermute | solution.py:37
  85.2 5.5 %collective-permute-start.9 = (bf16[48,1024]{1,0:T(8,128)(2,1)S(1)}, bf16[48,1024]{1,0:T(8,128)(2,1)S(1)}, u32[]{:S(2)}, u32[]{:S(2)}) collective-permute-start(bf16[48,1024]{1,0:T(8,128)(2,1)S(1)} %get-tuple-element.24), channel_id=1, source_target_pairs={{0,96},{8,104},{16,112},{24,120},{32,0},{40,8},{48,16},{56,24},{64... | collective-permute-start | bytes 294920 | tf_op jit(solution)/shard_map/ppermute | solution.py:37
  90.7 3.2 %collective-permute-done.7 = bf16[48,1024]{1,0:T(8,128)(2,1)S(1)} collective-permute-done((bf16[48,1024]{1,0:T(8,128)(2,1)S(1)}, bf16[48,1024]{1,0:T(8,128)(2,1)S(1)}, u32[]{:S(2)}, u32[]{:S(2)}) %collective-permute-start.7) | collective-permute-done | bytes 98336 | tf_op jit(solution)/shard_map/ppermute | solution.py:37
  93.9 5.8 %collective-permute-done.9 = bf16[48,1024]{1,0:T(8,128)(2,1)S(1)} collective-permute-done((bf16[48,1024]{1,0:T(8,128)(2,1)S(1)}, bf16[48,1024]{1,0:T(8,128)(2,1)S(1)}, u32[]{:S(2)}, u32[]{:S(2)}) %collective-permute-start.9) | collective-permute-done | bytes 98336 | tf_op jit(solution)/shard_map/ppermute | solution.py:37
  99.7 0.7 add_multiply_fusion
  (13 shorter events, 0.5 us)
Async XLA Ops:
  2.4 13.5 %all-to-all-start = ((bf16[4,32,768]{2,1,0:T(8,128)(2,1)}), bf16[4,32,768]{2,1,0:T(8,128)(2,1)S(1)}, u32[]{:S(2)}, u32[]{:S(2)}) async-start(bf16[4,32,768]{2,1,0:T(8,128)(2,1)} %pad_maximum_fusion.1), calls=%async_computation | async-start | bytes 393216 | tf_op jit(solution)/shard_map/all_to_all | solution.py:107
  15.8 12.3 %collective-permute-start.1 = (bf16[256,1024]{1,0:T(8,128)(2,1)S(1)}, bf16[256,1024]{1,0:T(8,128)(2,1)S(1)}, u32[]{:S(2)}, u32[]{:S(2)}) collective-permute-start(bf16[256,1024]{1,0:T(8,128)(2,1)S(1)} %bitcast.22), channel_id=1, source_target_pairs={{0,384},{128,0},{256,128},{384,256},{1,385},{129,1},{257,129},{385... | collective-permute-start | bytes 1572872 | tf_op jit(solution)/shard_map/ppermute | solution.py:28
  18.3 11.6 %collective-permute-start = (bf16[256,1024]{1,0:T(8,128)(2,1)S(1)}, bf16[256,1024]{1,0:T(8,128)(2,1)S(1)}, u32[]{:S(2)}, u32[]{:S(2)}) collective-permute-start(bf16[256,1024]{1,0:T(8,128)(2,1)S(1)} %bitcast.23), channel_id=1, source_target_pairs={{0,128},{128,256},{256,384},{384,0},{1,129},{129,257},{257,385},{3... | collective-permute-start | bytes 1572872 | tf_op jit(solution)/shard_map/ppermute | solution.py:28
  23.8 13.0 %all-to-all-start.1 = ((bf16[4,4,32,768]{3,2,1,0:T(8,128)(2,1)}), bf16[4,4,32,768]{3,2,1,0:T(8,128)(2,1)S(1)}, u32[]{:S(2)}, u32[]{:S(2)}) async-start(bf16[4,4,32,768]{3,2,1,0:T(8,128)(2,1)} %spread.1), calls=%async_computation.1 | async-start | bytes 1572864 | tf_op jit(solution)/shard_map/all_to_all | solution.py:129
  29.9 12.7 %collective-permute-start.3 = (bf16[256,1024]{1,0:T(8,128)(2,1)S(1)}, bf16[256,1024]{1,0:T(8,128)(2,1)S(1)}, u32[]{:S(2)}, u32[]{:S(2)}) collective-permute-start(bf16[256,1024]{1,0:T(8,128)(2,1)S(1)} %chosen.1), channel_id=1, source_target_pairs={{0,128},{1,385},{128,256},{129,1},{256,384},{257,129},{384,0},{385... | collective-permute-start | bytes 1572872 | tf_op jit(solution)/shard_map/ppermute | solution.py:33
  37.4 4.2 %collective-permute-start.2 = (bf16[512,768]{1,0:T(8,128)(2,1)S(1)}, bf16[512,768]{1,0:T(8,128)(2,1)S(1)}, u32[]{:S(2)}, u32[]{:S(2)}) collective-permute-start(bf16[512,768]{1,0:T(8,128)(2,1)S(1)} %ordered_rows.1), channel_id=1, source_target_pairs={{0,1},{1,0},{2,3},{3,2},{4,5},{5,4},{6,7},{7,6},{8,9},{9,8},{10,11... | collective-permute-start | bytes 2359304 | tf_op jit(solution)/shard_map/ppermute | solution.py:140
  43.4 18.8 %collective-permute-start.4 = (bf16[4,48,1024]{2,1,0:T(8,128)(2,1)S(1)}, bf16[4,48,1024]{2,1,0:T(8,128)(2,1)S(1)}, u32[]{:S(2)}, u32[]{:S(2)}) collective-permute-start(bf16[4,48,1024]{2,1,0:T(8,128)(2,1)S(1)} %get-tuple-element.18), channel_id=1, source_target_pairs={{0,16},{1,113},{8,24},{9,121},{16,32},{17,1},{24,40},{25,9},{32,48... | collective-permute-start | bytes 1179656 | tf_op jit(solution)/shard_map/ppermute | solution.py:42
  46.2 24.6 %collective-permute-start.5 = (bf16[4,48,1024]{2,1,0:T(8,128)(2,1)S(1)}, bf16[4,48,1024]{2,1,0:T(8,128)(2,1)S(1)}, u32[]{:S(2)}, u32[]{:S(2)}) collective-permute-start(bf16[4,48,1024]{2,1,0:T(8,128)(2,1)S(1)} %get-tuple-element.19), channel_id=1, source_target_pairs={{0,8},{8,16},{16,24},{24,32},{32,40},{40,48},{48,56},{56,64},{64,7... | collective-permute-start | bytes 1179656 | tf_op jit(solution)/shard_map/ppermute | solution.py:37
  50.1 20.8 %collective-permute-start.6 = (bf16[4,48,1024]{2,1,0:T(8,128)(2,1)S(1)}, bf16[4,48,1024]{2,1,0:T(8,128)(2,1)S(1)}, u32[]{:S(2)}, u32[]{:S(2)}) collective-permute-start(bf16[4,48,1024]{2,1,0:T(8,128)(2,1)S(1)} %get-tuple-element.20), channel_id=1, source_target_pairs={{0,120},{8,0},{16,8},{24,16},{32,24},{40,32},{48,40},{56,48},{64,5... | collective-permute-start | bytes 1179656 | tf_op jit(solution)/shard_map/ppermute | solution.py:37
  71.0 22.9 %collective-permute-start.7 = (bf16[48,1024]{1,0:T(8,128)(2,1)S(1)}, bf16[48,1024]{1,0:T(8,128)(2,1)S(1)}, u32[]{:S(2)}, u32[]{:S(2)}) collective-permute-start(bf16[48,1024]{1,0:T(8,128)(2,1)S(1)} %get-tuple-element.22), channel_id=1, source_target_pairs={{0,64},{8,72},{16,80},{24,88},{32,96},{40,104},{48,112},{56,120},{... | collective-permute-start | bytes 294920 | tf_op jit(solution)/shard_map/ppermute | solution.py:37
  80.9 13.0 %collective-permute-start.8 = (bf16[48,1024]{1,0:T(8,128)(2,1)S(1)}, bf16[48,1024]{1,0:T(8,128)(2,1)S(1)}, u32[]{:S(2)}, u32[]{:S(2)}) collective-permute-start(bf16[48,1024]{1,0:T(8,128)(2,1)S(1)} %get-tuple-element.23), channel_id=1, source_target_pairs={{0,32},{8,40},{16,48},{24,56},{32,64},{40,72},{48,80},{56,88},{64,... | collective-permute-start | bytes 294920 | tf_op jit(solution)/shard_map/ppermute | solution.py:37
  85.2 14.5 %collective-permute-start.9 = (bf16[48,1024]{1,0:T(8,128)(2,1)S(1)}, bf16[48,1024]{1,0:T(8,128)(2,1)S(1)}, u32[]{:S(2)}, u32[]{:S(2)}) collective-permute-start(bf16[48,1024]{1,0:T(8,128)(2,1)S(1)} %get-tuple-element.24), channel_id=1, source_target_pairs={{0,96},{8,104},{16,112},{24,120},{32,0},{40,8},{48,16},{56,24},{64... | collective-permute-start | bytes 294920 | tf_op jit(solution)/shard_map/ppermute | solution.py:37
